TPU v7x, 256 devices: a whole 4x4x8 slice. The times are simulated.
256 devices in a mesh: row: 16 (over y, x_hi, core), col: 16 (over z, x_lo).
Axes of the slice: x: 4 (x_hi: 2, x_lo: 2; x = x_hi * 2 + x_lo), y: 4, z: 8, core: 2. Of those that a mesh axis runs over, the one named last changes fastest.
Arguments:
- amplitudes: bfloat16 [100, 100, 3072], P(None, None, 'col'), may hold values from -6 to 6
- integrals: bfloat16 [3072, 262144], P('col', 'row'), may hold values from -0.078125 to 0.078125
- blocks: int32 [32, 2], replicated, may hold values from 0 to 49, as said below
Outputs:
- residual: bfloat16 [128, 262144], P('col', 'row')
Inputs may be any that keep to these rules, and one draw needn't show every extreme that they name: `blocks`: each row is a block pair (I, J) with I <= J, all rows distinct; the pair (0, 49) is always among them.
All inputs are finite; a program needn't handle non-finite values.
Results may differ from a plain program's by a relative error of at most 0.001.
Values may be sent and summed in bfloat16 or wider, within the bound.
No kernel may reach another device: no remote copies, remote signals or barrier semaphores. Data moves between devices by JAX's collectives and lax.ppermute only.
A program may use at most 128 MiB of HBM per device.

v0:
```python
import jax
import jax.numpy as jnp
from jax import lax
from jax.sharding import PartitionSpec as P

OB = 2
A_DEV = 32


def pick_rows(amplitudes, blocks):
    panel_width = amplitudes.shape[2]

    def one_block(pair_index):
        first_row = pair_index[0] * OB
        second_row = pair_index[1] * OB
        anchor = jnp.zeros((), jnp.int32)
        direct_rows = lax.dynamic_slice(
            amplitudes, (first_row, second_row, anchor), (OB, OB, panel_width)
        )
        swapped_rows = lax.dynamic_slice(
            amplitudes, (second_row, first_row, anchor), (OB, OB, panel_width)
        )
        return (
            direct_rows.reshape(OB * OB, panel_width),
            jnp.swapaxes(swapped_rows, 0, 1).reshape(OB * OB, panel_width),
        )

    direct_rows, swapped_rows = jax.vmap(one_block)(blocks)
    return (direct_rows.reshape(-1, panel_width), swapped_rows.reshape(-1, panel_width))


def on_device(amplitudes, integrals, blocks):
    forward, mirrored = pick_rows(amplitudes, blocks)
    depth = integrals.shape[0]
    full_width = integrals.shape[1] // A_DEV
    shaped = integrals.reshape(depth, A_DEV, full_width)
    received = lax.all_to_all(shaped, "row", split_axis=2, concat_axis=1, tiled=True)
    flipped = jnp.swapaxes(received, 1, 2).reshape(depth, A_DEV * full_width)
    summed = lax.psum_scatter(
        jnp.dot(forward, integrals, preferred_element_type=jnp.float32)
        + jnp.dot(mirrored, flipped, preferred_element_type=jnp.float32),
        "col",
        scatter_dimension=0,
        tiled=True,
    )
    return summed.astype(jnp.bfloat16)


def solution(mesh):
    return jax.shard_map(
        on_device,
        mesh=mesh,
        in_specs=(P(None, None, "col"), P("col", "row"), P()),
        out_specs=P("col", "row"),
        check_vma=False,
    )
```

profile of v0, /device:TPU:1, one launch (start us, length us, event | category | flops | bytes accessed | tf_op | source)
XLA Modules:
  0.0 473.7 jit_solution(13747249918795934417)
XLA Ops:
  6.5 8.2 %copy.23 = bf16[24,8,32,512]{3,2,1,0:T(8,128)(2,1)} copy(bf16[24,8,32,512]{3,1,2,0:T(8,128)(2,1)} %bitcast.35) | data formatting | bytes 12582912
  14.8 15.1 %copy.16 = bf16[192,32,512]{0,1,2:T(8,128)(2,1)} copy(bf16[192,32,512]{2,1,0:T(8,128)(2,1)} %bitcast.38) | data formatting | bytes 12582912 | tf_op jit(solution)/shard_map/reshape | solution.py:36
  29.9 8.6 %all-to-all-start = ((bf16[192,32,512]{0,1,2:T(8,128)(2,1)}), bf16[192,32,512]{0,1,2:T(8,128)(2,1)}, u32[]{:S(2)}, u32[]{:S(2)}) async-start(bf16[192,32,512]{0,1,2:T(8,128)(2,1)} %copy.16), calls=%async_computation | async-start | bytes 16777216 | tf_op jit(solution)/shard_map/all_to_all | solution.py:37
  38.8 97.5 %while.2 = (s32[]{:T(128)}, bf16[100,100,192]{1,2,0:T(8,128)(2,1)}, s32[32,3]{0,1:T(4,128)S(1)}, bf16[32,2,2,192]{3,2,1,0:T(2,128)(2,1)S(1)}, s32[]{:T(128)}) while((s32[]{:T(128)}, bf16[100,100,192]{1,2,0:T(8,128)(2,1)}, s32[32,3]{0,1:T(4,128)S(1)}, bf16[32,2,2,192]{3,2,1,0:T(2,128)(2,1)S(1)}, s32[]{:T(128)}) %tuple.35), condition=%wide.while_cond, body=%wide.while_body.sunk | while | flops 2 | bytes 10365 | solution.py:17
  136.3 93.4 %while.3 = (s32[]{:T(128)}, bf16[100,100,192]{1,2,0:T(8,128)(2,1)}, s32[32,3]{0,1:T(4,128)S(1)}, bf16[32,2,2,192]{2,3,1,0:T(8,128)(2,1)S(1)}, s32[]{:T(128)}) while((s32[]{:T(128)}, bf16[100,100,192]{1,2,0:T(8,128)(2,1)}, s32[32,3]{0,1:T(4,128)S(1)}, bf16[32,2,2,192]{2,3,1,0:T(8,128)(2,1)S(1)}, s32[]{:T(128)}) %tuple.43), condition=%wide.while_cond.1, body=%wide.while_body.1.sunk | while | flops 2 | bytes 99965 | solution.py:20
  136.9 2.3 bitcast_dynamic-update-slice_fusion.2
  139.8 2.3 bitcast_dynamic-update-slice_fusion.2
  142.8 2.3 bitcast_dynamic-update-slice_fusion.2
  145.7 2.3 bitcast_dynamic-update-slice_fusion.2
  148.6 2.3 bitcast_dynamic-update-slice_fusion.2
  151.5 2.3 bitcast_dynamic-update-slice_fusion.2
  154.4 2.3 bitcast_dynamic-update-slice_fusion.2
  157.4 2.3 bitcast_dynamic-update-slice_fusion.2
  160.3 2.3 bitcast_dynamic-update-slice_fusion.2
  163.2 2.3 bitcast_dynamic-update-slice_fusion.2
  166.1 2.3 bitcast_dynamic-update-slice_fusion.2
  169.0 2.3 bitcast_dynamic-update-slice_fusion.2
  172.0 2.3 bitcast_dynamic-update-slice_fusion.2
  174.9 2.3 bitcast_dynamic-update-slice_fusion.2
  177.8 2.3 bitcast_dynamic-update-slice_fusion.2
  180.7 2.3 bitcast_dynamic-update-slice_fusion.2
  183.6 2.3 bitcast_dynamic-update-slice_fusion.2
  186.6 2.3 bitcast_dynamic-update-slice_fusion.2
  189.5 2.3 bitcast_dynamic-update-slice_fusion.2
  192.4 2.3 bitcast_dynamic-update-slice_fusion.2
  229.8 2.7 copy.15
  232.6 7.3 %fusion.2 = f32[128,16384]{1,0:T(8,128)} fusion(bf16[128,192]{1,0:T(8,128)(2,1)S(1)} %reshape.12, bf16[192,16384]{1,0:T(8,128)(2,1)} %param.4), kind=kOutput, calls=%fused_computation.12 | convolution fusion | flops 805306368 | bytes 14729216 | tf_op jit(solution)/shard_map/dot_general | solution.py:40
  239.8 12.3 %copy.18 = bf16[192,16,32,32]{0,3,2,1:T(8,128)(2,1)} copy(bf16[192,16,32,32]{0,2,3,1:T(8,128)(2,1)} %bitcast.3) | data formatting | bytes 12582912 | tf_op jit(solution)/shard_map/all_to_all | solution.py:37
  252.2 15.4 %copy.19 = bf16[192,32,512]{2,1,0:T(8,128)(2,1)} copy(bf16[192,32,512]{0,1,2:T(8,128)(2,1)} %bitcast.36) | data formatting | bytes 12582912 | tf_op jit(solution)/shard_map/transpose | solution.py:38
  267.5 7.5 %copy.24 = bf16[24,8,32,512]{3,1,2,0:T(8,128)(2,1)S(1)} copy(bf16[24,8,32,512]{3,2,1,0:T(8,128)(2,1)} %bitcast.37) | data formatting | bytes 12582912
  275.1 4.6 convolution_add_fusion
  279.7 185.4 %reduce-scatter.2.cloned.1.call-done = f32[8,16384]{1,0:T(8,128)} async-done(((f32[128,16384]{1,0:T(8,128)}), f32[8,16384]{1,0:T(8,128)}) %reduce-scatter.2.cloned.1.call-update) | async-done | bytes 524304 | tf_op jit(solution)/shard_map/reduce_scatter | solution.py:39
  (251 shorter events, 146.0 us)
Async XLA Ops:
  29.9 8.8 %copy-start.1 = (s32[32,2]{0,1:T(2,128)S(1)}, s32[32,2]{0,1:T(2,128)}, u32[]{:S(2)}) copy-start(s32[32,2]{0,1:T(2,128)} %param.5) | copy-start | bytes 772
  29.9 210.0 %all-to-all-start = ((bf16[192,32,512]{0,1,2:T(8,128)(2,1)}), bf16[192,32,512]{0,1,2:T(8,128)(2,1)}, u32[]{:S(2)}, u32[]{:S(2)}) async-start(bf16[192,32,512]{0,1,2:T(8,128)(2,1)} %copy.16), calls=%async_computation | async-start | bytes 16777216 | tf_op jit(solution)/shard_map/all_to_all | solution.py:37
  38.5 426.6 %reduce-scatter.2.cloned.1.call-start = ((), (), s32[]{:S(2)}) async-start(), calls=%async_computation.2 | async-start | bytes 8912896 | tf_op jit(solution)/shard_map/reduce_scatter | solution.py:39
  267.5 7.5 %copy-start = (f32[128,16384]{1,0:T(8,128)S(1)}, f32[128,16384]{1,0:T(8,128)}, u32[]{:S(2)}) copy-start(f32[128,16384]{1,0:T(8,128)} %fusion.2) | copy-start | bytes 25165828
Sparse Core Ops, SparseCore 0:
  279.8 185.2 reduce-scatter.1
where the time goes:
time: 478 us; the launch traced here: 474 us
  local copies, waits for them, and re-layouts  251 us (53%)
  waiting for transfers between devices  185 us (39%)
  between operations  13.5 us (3%)
  matrix products  11.8 us (2%)
  starting transfers between devices  8.79 us (2%)
    gather x256, local copies, waits for them, and re-layouts  190 us
    reduce_scatter x1, waiting for transfers between devices, on_device(): lax.psum_scatter(jnp.dot(forward, integrals, preferred_element_type=jnp.f...  185 us
    unnamed x6, local copies, waits for them, and re-layouts  15.8 us
    transpose x1, local copies, waits for them, and re-layouts, on_device(): flipped = jnp.swapaxes(received, 1, 2).reshape(depth, A_DEV * full_width)  15.4 us
    reshape x1, local copies, waits for them, and re-layouts, on_device(): shaped = integrals.reshape(depth, A_DEV, full_width)  15.1 us
    all_to_all x1, local copies, waits for them, and re-layouts, on_device(): lax.all_to_all(shaped, 'row', split_axis=2, concat_axis=1, tiled=True)  12.3 us
  transfers between devices with their start and end apart: 2, of which 1 were waited for; matrix products, arithmetic and copies ran while one was open for 42% of the time, Pallas kernels for 0%

commit v1 on v0

v1 whole, which is shorter than its diff:
```python
import functools

import jax
import jax.numpy as jnp
from jax import lax
from jax.experimental import pallas as pl
from jax.experimental.pallas import tpu as pltpu
from jax.sharding import Mesh
from jax.sharding import PartitionSpec as P

OB = 2
PB = OB * OB
A_DEV = 32
AW = 512
F32, I16 = jnp.float32, jnp.int16
ROW, Z, XL = "row", "z", "xl"
LANES = 128
TILES = A_DEV * AW // (16 * LANES)
ROW_W = TILES * LANES
TOP = 32700.0
STEPS = 256.0


def params(mib=32):
    return pltpu.CompilerParams(vmem_limit_bytes=mib << 20)


def cost(flops, bytes_accessed):
    return pl.CostEstimate(flops=flops, bytes_accessed=bytes_accessed, transcendentals=0)


def vmem():
    return pl.BlockSpec(memory_space=pltpu.VMEM)


def scale_of(tiles):
    most = functools.reduce(jnp.maximum, [jnp.abs(t) for t in tiles])
    most = jnp.max(most, axis=0, keepdims=True)
    code = jnp.ceil(jnp.log2(jnp.maximum(most, 2.0**-100)) * STEPS)
    return code, TOP * jnp.exp2(code * (-1.0 / STEPS))


def coded(x, factor):
    return jnp.round(x * factor).astype(jnp.int32).astype(I16)


def factors(codes):
    return jnp.exp2(codes.astype(F32) * (1.0 / STEPS)) * (1.0 / TOP)


def column(k, n):
    return k * ROW_W + (LANES if k >= n // 2 else 0)


def get_row(ref, start, factor):
    return [
        ref[:, start + t * LANES : start + (t + 1) * LANES].astype(jnp.int32).astype(F32) * factor
        for t in range(TILES)
    ]


def put_row(ref, start, tiles):
    code, factor = scale_of(tiles)
    for t, tile in enumerate(tiles):
        ref[:, start + t * LANES : start + (t + 1) * LANES] = coded(tile, factor)
    return code


def scale_tile(codes):
    rows = codes + [jnp.zeros((1, LANES), F32)] * (16 - len(codes))
    return jnp.concatenate(rows, axis=0).astype(jnp.int32).astype(I16)


def gather_kernel(blocks, pages, out, padded, picked):
    depth, orbitals = pages.shape[1], pages.shape[2]
    pairs = blocks.shape[0]
    lane = lax.broadcasted_iota(jnp.int32, (depth, LANES), 1)
    padded[...] = jnp.zeros_like(padded)
    picked[...] = jnp.zeros_like(picked)

    def one(pair, _):
        first, second = blocks[pair, 0] * OB, blocks[pair, 1] * OB
        base = pair * PB
        for s in range(OB):
            padded[0, :, :orbitals] = pages[first + s].astype(F32)
            padded[1, :, :orbitals] = pages[second + s].astype(F32)
            to = base + s * OB
            here = (lane >= to) & (lane < to + OB)
            picked[0] = jnp.where(here, pltpu.roll(padded[0], lax.rem(to - second + LANES, LANES), 1), picked[0])
            picked[1] = jnp.where(here, pltpu.roll(padded[1], lax.rem(to - first + LANES, LANES), 1), picked[1])
        return 0

    lax.fori_loop(0, pairs, one, 0)
    mirrored = picked[1]
    which = lax.rem(lane, PB)
    mirrored = jnp.where(
        which == 1, pltpu.roll(mirrored, LANES - 1, 1), jnp.where(which == 2, pltpu.roll(mirrored, 1, 1), mirrored)
    )
    out[0] = picked[0].T.astype(out.dtype)
    out[1] = mirrored.T.astype(out.dtype)


def gather(amplitudes, blocks):
    depth = amplitudes.shape[2]
    rows = blocks.shape[0] * PB
    return pl.pallas_call(
        gather_kernel,
        out_shape=jax.ShapeDtypeStruct((2, rows, depth), jnp.bfloat16),
        in_specs=[pl.BlockSpec(memory_space=pltpu.SMEM), vmem()],
        out_specs=vmem(),
        scratch_shapes=[pltpu.VMEM((2, depth, LANES), F32), pltpu.VMEM((2, depth, LANES), F32)],
        compiler_params=params(24),
        name="pick_rows",
    )(blocks, jnp.swapaxes(amplitudes, 1, 2))


GRID = 8


def product_kernel(z_n, n, left, right, out, whole):
    step = pl.program_id(0)
    rows = left.shape[0]
    each = A_DEV // GRID
    for i in range(each):
        part = jnp.dot(left[...], right[:, i * AW : (i + 1) * AW], preferred_element_type=F32)
        for c in range(AW // LANES):
            whole[c, pl.ds(step * each + i, rows, stride=A_DEV), :] = part[:, c * LANES : (c + 1) * LANES]

    @pl.when(step == GRID - 1)
    def _():
        def one(z, _):
            codes = []
            for k in range(n):
                tiles = [
                    whole[c, pl.ds(pl.multiple_of((z * n + k) * A_DEV + h * 16, 16), 16), :]
                    for h in range(2)
                    for c in range(AW // LANES)
                ]
                codes.append(put_row(out.at[z], column(k, n), tiles))
            out[z, :, column(n // 2, n) - LANES : column(n // 2, n)] = scale_tile(codes)
            return 0

        lax.fori_loop(0, z_n, one, 0)


def product(left, integrals, z_n):
    rows, depth = left.shape
    n = rows // z_n
    width = integrals.shape[1]
    return pl.pallas_call(
        functools.partial(product_kernel, z_n, n),
        grid=(GRID,),
        out_shape=jax.ShapeDtypeStruct((z_n, 16, n * ROW_W + LANES), I16),
        in_specs=[
            pl.BlockSpec((rows, depth), lambda s: (0, 0)),
            pl.BlockSpec((depth, width // GRID), lambda s: (0, s)),
        ],
        out_specs=pl.BlockSpec((z_n, 16, n * ROW_W + LANES), lambda s: (0, 0, 0)),
        scratch_shapes=[pltpu.VMEM((AW // LANES, rows * A_DEV, LANES), F32)],
        compiler_params=params(40),
        cost_estimate=cost(2 * rows * depth * width, 2 * depth * width + 2 * rows * width),
        name="product",
    )(left, integrals)


def step_kernel(n, first, at, got_r, got_l, own_r, own_l, out_r, out_l):
    half = n // 2
    middle = half * ROW_W
    for side, got, own, out in ((0, got_r, own_r, out_r), (1, got_l, own_l, out_l)):
        own_codes = own[0, :, middle : middle + LANES].astype(jnp.int32).astype(F32)
        own_f = factors(own_codes)
        if first:
            spot = middle if side == 0 else 0
            got_f = factors(got[:, spot : spot + LANES].astype(jnp.int32))
        else:
            got_f = factors(got[:, middle : middle + LANES].astype(jnp.int32))
        codes = []
        for k in range(n):
            start = column(k, n)
            if first and (k < half) != (side == 0):
                out[:, start : start + ROW_W] = own[0, :, start : start + ROW_W]
                codes.append(own_codes[k : k + 1])
                continue
            came = start - (middle if first and side == 1 else 0)
            a = get_row(got, came, got_f[k : k + 1])
            b = get_row(own.at[0], start, own_f[k : k + 1])
            codes.append(put_row(out, start, [x + y for x, y in zip(a, b)]))
        out[:, middle : middle + LANES] = scale_tile(codes)


def ring_step(got_r, got_l, parts, at, n, first):
    z_n, _, width = parts.shape
    shape = jax.ShapeDtypeStruct((16, width), I16)
    whole = lambda shape: pl.BlockSpec(shape, lambda s, at: (0, 0))
    return pl.pallas_call(
        functools.partial(step_kernel, n, first),
        out_shape=(shape, shape),
        grid_spec=pltpu.PrefetchScalarGridSpec(
            num_scalar_prefetch=1,
            grid=(1,),
            in_specs=[
                whole(got_r.shape),
                whole(got_l.shape),
                pl.BlockSpec((1, 16, width), lambda s, at: (at[0], 0, 0)),
                pl.BlockSpec((1, 16, width), lambda s, at: (at[1], 0, 0)),
            ],
            out_specs=[whole((16, width)), whole((16, width))],
        ),
        compiler_params=params(16),
        cost_estimate=cost(16 * width * 8, 16 * width * 12),
        name="ring_step",
    )(at, got_r, got_l, parts, parts)


def ring(parts, n):
    z_n = parts.shape[0]
    me = lax.axis_index(Z)
    right = [(i, (i + 1) % z_n) for i in range(z_n)]
    left = [((i + 1) % z_n, i) for i in range(z_n)]
    middle = n // 2 * ROW_W
    far = z_n // 2
    opposite = lax.dynamic_index_in_dim(parts, lax.rem(me + far, z_n), 0, keepdims=False)
    r, l = opposite[:, : middle + LANES], opposite[:, middle:]
    for d in range(far, 0, -1):
        r = lax.ppermute(r, Z, right)
        l = lax.ppermute(l, Z, left)
        if d > 1:
            at = jnp.stack([lax.rem(me + d - 1, z_n), lax.rem(me + z_n - d + 1, z_n)])
            r, l = ring_step(r, l, parts, at, n, d == far)
    return r, l


def end_rows(n, refs, starts_at):
    middle = n // 2 * ROW_W
    f = [factors(ref[:, middle : middle + LANES].astype(jnp.int32)) for ref in refs]

    def row(k):
        rows = [get_row(ref, column(k, n), g[k : k + 1]) for ref, g in zip(refs, f)]
        return [x + y + w for x, y, w in zip(*rows)]

    return row


def matrix(tiles):
    per = len(tiles) // 2
    return jnp.concatenate(
        [jnp.concatenate(tiles[:per], axis=1), jnp.concatenate(tiles[per:], axis=1)], axis=0
    )


def turn_kernel(n, rows_n, at, got_r, got_l, own, out):
    row = end_rows(n, [got_r, got_l, own.at[0]], None)
    groups = n // (2 * PB)
    for xl in range(2):
        codes = []
        for g in range(groups):
            stack = jnp.concatenate([matrix(row((xl * groups + g) * PB + i)) for i in range(PB)], axis=0)
            turned = stack.T
            code, factor = scale_of([turned])
            codes.append(code)
            for to in range(rows_n):
                out[to, xl, g * A_DEV : (g + 1) * A_DEV, :] = coded(turned[to * A_DEV : (to + 1) * A_DEV], factor)
        tile = scale_tile(codes)
        for to in range(rows_n):
            out[to, xl, groups * A_DEV : groups * A_DEV + 16, :] = tile


def turn(got_r, got_l, parts, n, rows_n):
    z_n, _, width = parts.shape
    whole = lambda shape: pl.BlockSpec(shape, lambda s, at: (0,) * len(shape))
    shape = (rows_n, 2, n // (2 * PB) * A_DEV + 16, LANES)
    return pl.pallas_call(
        functools.partial(turn_kernel, n, rows_n),
        out_shape=jax.ShapeDtypeStruct(shape, I16),
        grid_spec=pltpu.PrefetchScalarGridSpec(
            num_scalar_prefetch=1,
            grid=(1,),
            in_specs=[
                whole((16, width)),
                whole((16, width)),
                pl.BlockSpec((1, 16, width), lambda s, at: (at[0], 0, 0)),
            ],
            out_specs=whole(shape),
        ),
        compiler_params=params(32),
        cost_estimate=cost(16 * width * 8, 16 * width * 8),
        name="turn",
    )(lax.axis_index(Z)[None], got_r, got_l, parts)


def share_kernel(n, at, got_r, got_l, own, keep, give):
    row = end_rows(n, [got_r, got_l, own.at[0]], None)
    half = n // 2
    first = at[1] == 0
    codes = []
    for i in range(half):
        low, high = row(i), row(half + i)
        keep[i] = matrix([jnp.where(first, a, b) for a, b in zip(low, high)])
        codes.append(put_row(give, column(i, half), [jnp.where(first, b, a) for a, b in zip(low, high)]))
    give[:, column(half // 2, half) - LANES : column(half // 2, half)] = scale_tile(codes)


def share(got_r, got_l, parts, n):
    z_n, _, width = parts.shape
    half = n // 2
    whole = lambda shape: pl.BlockSpec(shape, lambda s, at: (0,) * len(shape))
    return pl.pallas_call(
        functools.partial(share_kernel, n),
        out_shape=(
            jax.ShapeDtypeStruct((half, A_DEV, AW), F32),
            jax.ShapeDtypeStruct((16, half * ROW_W + LANES), I16),
        ),
        grid_spec=pltpu.PrefetchScalarGridSpec(
            num_scalar_prefetch=1,
            grid=(1,),
            in_specs=[
                whole((16, width)),
                whole((16, width)),
                pl.BlockSpec((1, 16, width), lambda s, at: (at[0], 0, 0)),
            ],
            out_specs=[whole((half, A_DEV, AW)), whole((16, half * ROW_W + LANES))],
        ),
        compiler_params=params(16),
        cost_estimate=cost(16 * width * 8, 16 * width * 8),
        name="share",
    )(jnp.stack([lax.axis_index(Z), lax.axis_index(XL)]), got_r, got_l, parts)


def regroup(tiles):
    count = len(tiles)
    group = LANES // count
    lane = lax.broadcasted_iota(jnp.int32, tiles[0].shape, 1) // group
    out = []
    for k in range(count):
        merged = tiles[k]
        for r in range(count):
            if r != k:
                merged = jnp.where(lane == r, pltpu.roll(tiles[r], (r - k) % count * group, 1), merged)
        out.append(merged)
    return out


def last_kernel(n, rows_n, mirrored, keep, got, out, total):
    half = n // 2
    groups = half // PB
    at = groups * A_DEV
    f = [[factors(mirrored[r, s, at : at + 16, :].astype(jnp.int32)) for s in range(2)] for r in range(rows_n)]
    middle = half // 2 * ROW_W
    got_f = factors(got[:, middle : middle + LANES].astype(jnp.int32))
    for g in range(groups):
        pieces = []
        for r in range(rows_n):
            both = [
                mirrored[r, s, g * A_DEV : (g + 1) * A_DEV, :].astype(jnp.int32).astype(F32) * f[r][s][g : g + 1]
                for s in range(2)
            ]
            pieces.append(both[0] + both[1])
        per = LANES // A_DEV
        for c in range(rows_n // per):
            for i, tile in enumerate(regroup(pieces[c * per : (c + 1) * per])):
                total[c, pl.ds((g * PB + i) * A_DEV, A_DEV), :] = tile
    for k in range(half):
        tiles = get_row(got, column(k, half), got_f[k : k + 1])
        for h in range(2):
            for c in range(AW // LANES):
                lanes = slice(c * LANES, (c + 1) * LANES)
                spot = pl.ds(k * A_DEV + h * 16, 16)
                total[c, spot, :] += tiles[h * (AW // LANES) + c] + keep[k, h * 16 : (h + 1) * 16, lanes]
    for a in range(A_DEV):
        for c in range(AW // LANES):
            start = a * AW + c * LANES
            out[:, start : start + LANES] = total[c, pl.ds(a, half, stride=A_DEV), :].astype(out.dtype)


def last(mirrored, keep, got, n):
    half = n // 2
    rows_n = mirrored.shape[0]
    return pl.pallas_call(
        functools.partial(last_kernel, n, rows_n),
        out_shape=jax.ShapeDtypeStruct((half, A_DEV * AW), jnp.bfloat16),
        in_specs=[vmem()] * 3,
        out_specs=vmem(),
        scratch_shapes=[pltpu.VMEM((AW // LANES, half * A_DEV, LANES), F32)],
        compiler_params=params(16),
        name="last",
    )(mirrored, keep, got)


def on_device(rows_n, z_n, amplitudes, integrals, blocks):
    picked = gather(amplitudes, blocks)
    n = picked.shape[1] // z_n
    mirrored = product(picked[1], integrals, z_n)
    forward = product(picked[0], integrals, z_n)
    m_r, m_l = ring(mirrored, n)
    f_r, f_l = ring(forward, n)
    pieces = turn(m_r, m_l, mirrored, n, rows_n)
    shape = pieces.shape
    pieces = pieces.reshape((rows_n * 2,) + shape[2:])
    pieces = lax.all_to_all(pieces, (ROW, XL), 0, 0, tiled=True).reshape(shape)
    keep, give = share(f_r, f_l, forward, n)
    got = lax.ppermute(give, XL, [(0, 1), (1, 0)])
    return last(pieces, keep, got, n)


def solution(mesh):
    rows_n, cols_n = mesh.devices.shape
    finer = Mesh(mesh.devices.reshape(rows_n, cols_n // 2, 2), (ROW, Z, XL))
    return jax.shard_map(
        functools.partial(on_device, rows_n, cols_n // 2),
        mesh=finer,
        in_specs=(P(None, None, (Z, XL)), P((Z, XL), ROW), P()),
        out_specs=P((Z, XL), ROW),
        check_vma=False,
    )
```

time: 478 us -> 154 us (0.32)
  local copies, waits for them, and re-layouts: 251 us -> 23 us
  waiting for transfers between devices: 185 us -> 46.2 us
  Pallas kernels: 0 us -> 44.9 us
  starting transfers between devices: 8.79 us -> 39.4 us
  between operations: 13.5 us -> 0.24 us
  matrix products: 11.8 us -> 0 us
    gather x256 -> x0, local copies, waits for them, and re-layouts: 190 us -> none
    reduce_scatter x1 -> x0, waiting for transfers between devices: 185 us -> none  [on_device(): lax.psum_scatter(jnp.dot(forward, integrals, preferred_element_type=jnp.f...]
    ppermute x0 -> x17, waiting for transfers between devices: none -> 46.2 us  [the longest x8 36 us: ring(): r = lax.ppermute(r, Z, right)]
    pallas_call x0 -> x12, Pallas kernels: none -> 44.9 us  [the longest x2 24.6 us: product(): pl.pallas_call(functools.partial(product_kernel, z_n, n), grid=(GRID,), o...]
    ppermute x0 -> x17, starting transfers between devices: none -> 27.1 us  [the longest x8 19.7 us: ring(): l = lax.ppermute(l, Z, left)]
    transpose x2 -> x0, local copies, waits for them, and re-layouts: 18 us -> none  [the longest x1 15.4 us: on_device(): flipped = jnp.swapaxes(received, 1, 2).reshape(depth, A_DEV * full_width)]
    reshape x3 -> x0, local copies, waits for them, and re-layouts: 15.2 us -> none  [the longest x1 15.1 us: on_device(): shaped = integrals.reshape(depth, A_DEV, full_width)]
    all_to_all x1 -> x0, local copies, waits for them, and re-layouts: 12.3 us -> none  [on_device(): lax.all_to_all(shaped, 'row', split_axis=2, concat_axis=1, tiled=True)]
  transfers between devices with their start and end apart: 2 -> 18, of which waited for: 1 -> 6; matrix products, arithmetic and copies ran while one was open for 42% -> 0% of each run, Pallas kernels for 0% -> 15%
where the time goes in v1:
time: 154 us
  waiting for transfers between devices  46.2 us (30%)
  Pallas kernels  44.9 us (29%)
  starting transfers between devices  39.4 us (26%)
  local copies, waits for them, and re-layouts  23 us (15%)
    ppermute x8, waiting for transfers between devices, ring(): r = lax.ppermute(r, Z, right)  36 us
    pallas_call x2, Pallas kernels, product(): pl.pallas_call(functools.partial(product_kernel, z_n, n), grid=(GRID,), o...  24.6 us
    unnamed x35, local copies, waits for them, and re-layouts  21.8 us
    ppermute x8, starting transfers between devices, ring(): l = lax.ppermute(l, Z, left)  19.7 us
    all_to_all x1, starting transfers between devices, on_device(): pieces = lax.all_to_all(pieces, (ROW, XL), 0, 0, tiled=True).reshape(shape)  12.3 us
    ppermute x1, waiting for transfers between devices, on_device(): got = lax.ppermute(give, XL, [(0, 1), (1, 0)])  10.1 us
    pallas_call x6, Pallas kernels, ring_step(): pl.pallas_call(functools.partial(step_kernel, n, first), out_shape=(shape...  9.55 us
    pallas_call x1, Pallas kernels, gather(): pl.pallas_call(gather_kernel, out_shape=jax.ShapeDtypeStruct((2, rows, de...  6.76 us
  transfers between devices with their start and end apart: 18, of which 6 were waited for; matrix products, arithmetic and copies ran while one was open for 0% of the time, Pallas kernels for 15%

profile of v1, /device:TPU:1, one launch (start us, length us, event | category | flops | bytes accessed | tf_op | source)
XLA Modules:
  0.0 154.0 jit_solution(13234345317237328066)
XLA Ops:
  0.8 2.4 %copy-done.8 = bf16[100,100,192]{1,2,0:T(8,128)(2,1)S(1)} copy-done((bf16[100,100,192]{1,2,0:T(8,128)(2,1)S(1)}, bf16[100,100,192]{1,2,0:T(8,128)(2,1)}, u32[]{:S(2)}) %copy-start.8) | copy-done | bytes 3840024
  3.2 6.8 %pick_rows.1 = bf16[2,128,192]{2,1,0:T(8,128)(2,1)S(1)} custom-call(s32[32,2]{1,0:T(8,128)S(1)} %copy.4.blocks, bf16[100,192,100]{2,1,0:T(8,128)(2,1)S(1)} %bitcast.27), custom_call_target="tpu_custom_call" | custom-call | tf_op jit(solution)/shard_map/pick_rows/pallas_call | solution.py:106
  10.0 2.8 %copy-done.6 = bf16[192,16384]{1,0:T(8,128)(2,1)S(1)} copy-done((bf16[192,16384]{1,0:T(8,128)(2,1)S(1)}, bf16[192,16384]{1,0:T(8,128)(2,1)}, u32[]{:S(2)}) %copy-start.6) | copy-done | bytes 6291480
  12.7 12.3 %product.2.own_r.own_l.own = s16[8,16,16512]{2,1,0:T(8,128)(2,1)S(1)} custom-call(bf16[128,192]{1,0:T(8,128)(2,1)S(1)} %get-tuple-element.38.left, bf16[192,16384]{1,0:T(8,128)(2,1)S(1)} %copy-done.6), custom_call_target="tpu_custom_call" | custom-call | flops 805306368 | bytes 10485760 | tf_op jit(solution)/shard_map/product/pallas_call | solution.py:150
  25.1 2.0 %copy-done.2 = s16[8,16,16512]{2,1,0:T(8,128)(2,1)} copy-done((s16[8,16,16512]{2,1,0:T(8,128)(2,1)}, s16[8,16,16512]{2,1,0:T(8,128)(2,1)S(1)}, u32[]{:S(2)}) %copy-start.2) | copy-done | bytes 4227096
  28.2 2.5 %collective-permute-start = (s16[16,8320]{1,0:T(8,128)(2,1)S(1)}, s16[16,8320]{1,0:T(8,128)(2,1)S(1)}, u32[]{:S(2)}, u32[]{:S(2)}) collective-permute-start(s16[16,8320]{1,0:T(8,128)(2,1)S(1)} %get-tuple-element.36), channel_id=1, source_target_pairs={{0,2},{2,4},{4,6},{6,8},{8,10},{10,12},{12,14},{14,0},{1,3},{3,5},... | collective-permute-start | bytes 798728 | tf_op jit(solution)/shard_map/ppermute | solution.py:225
  30.7 4.0 %collective-permute-start.1 = (s16[16,8320]{1,0:T(8,128)(2,1)S(1)}, s16[16,8320]{1,0:T(8,128)(2,1)S(1)}, u32[]{:S(2)}, u32[]{:S(2)}) collective-permute-start(s16[16,8320]{1,0:T(8,128)(2,1)S(1)} %get-tuple-element.35), channel_id=1, source_target_pairs={{2,0},{4,2},{6,4},{8,6},{10,8},{12,10},{14,12},{0,14},{3,1},{5,3},... | collective-permute-start | bytes 798728 | tf_op jit(solution)/shard_map/ppermute | solution.py:226
  34.7 2.8 %copy-done.7 = bf16[192,16384]{1,0:T(8,128)(2,1)S(1)} copy-done((bf16[192,16384]{1,0:T(8,128)(2,1)S(1)}, bf16[192,16384]{1,0:T(8,128)(2,1)}, u32[]{:S(2)}) %copy-start.7) | copy-done | bytes 6291480
  37.5 12.3 %product.3.own_r.own_l.own = s16[8,16,16512]{2,1,0:T(8,128)(2,1)S(1)} custom-call(bf16[128,192]{1,0:T(8,128)(2,1)S(1)} %get-tuple-element.37.left, bf16[192,16384]{1,0:T(8,128)(2,1)S(1)} %copy-done.7), custom_call_target="tpu_custom_call" | custom-call | flops 805306368 | bytes 10485760 | tf_op jit(solution)/shard_map/product/pallas_call | solution.py:150
  49.9 2.0 %copy-done = s16[8,16,16512]{2,1,0:T(8,128)(2,1)} copy-done((s16[8,16,16512]{2,1,0:T(8,128)(2,1)}, s16[8,16,16512]{2,1,0:T(8,128)(2,1)S(1)}, u32[]{:S(2)}) %copy-start) | copy-done | bytes 4227096
  52.0 2.3 %copy-done.3 = s16[8,16,16512]{2,1,0:T(8,128)(2,1)S(1)} copy-done((s16[8,16,16512]{2,1,0:T(8,128)(2,1)S(1)}, s16[8,16,16512]{2,1,0:T(8,128)(2,1)}, u32[]{:S(2)}) %copy-start.3) | copy-done | bytes 4227096
  55.4 2.7 %collective-permute-start.3 = (s16[16,16512]{1,0:T(8,128)(2,1)S(1)}, s16[16,16512]{1,0:T(8,128)(2,1)S(1)}, u32[]{:S(2)}, u32[]{:S(2)}) collective-permute-start(s16[16,16512]{1,0:T(8,128)(2,1)S(1)} %get-tuple-element.20), channel_id=1, source_target_pairs={{2,0},{4,2},{6,4},{8,6},{10,8},{12,10},{14,12},{0,14},{3,1},{5,3},... | collective-permute-start | bytes 1585160 | tf_op jit(solution)/shard_map/ppermute | solution.py:226
  58.2 2.7 %collective-permute-start.9 = (s16[16,8320]{1,0:T(8,128)(2,1)S(1)}, s16[16,8320]{1,0:T(8,128)(2,1)S(1)}, u32[]{:S(2)}, u32[]{:S(2)}) collective-permute-start(s16[16,8320]{1,0:T(8,128)(2,1)S(1)} %get-tuple-element.33), channel_id=1, source_target_pairs={{2,0},{4,2},{6,4},{8,6},{10,8},{12,10},{14,12},{0,14},{3,1},{5,3},... | collective-permute-start | bytes 798728 | tf_op jit(solution)/shard_map/ppermute | solution.py:226
  60.8 14.0 %collective-permute-done.8.got_r = s16[16,8320]{1,0:T(8,128)(2,1)S(1)} collective-permute-done((s16[16,8320]{1,0:T(8,128)(2,1)S(1)}, s16[16,8320]{1,0:T(8,128)(2,1)S(1)}, u32[]{:S(2)}, u32[]{:S(2)}) %collective-permute-start.8) | collective-permute-done | bytes 266272 | tf_op jit(solution)/shard_map/ppermute | solution.py:225
  74.8 1.9 %ring_step.9 = (s16[16,16512]{1,0:T(8,128)(2,1)}, s16[16,16512]{1,0:T(8,128)(2,1)}) custom-call(s32[2]{0:T(128)S(1)} %pad_add_fusion.2.at, s16[16,8320]{1,0:T(8,128)(2,1)S(1)} %collective-permute-done.8.got_r, s16[16,8320]{1,0:T(8,128)(2,1)S(1)} %collective-permute-done.9.got_l, s16[8,16,16512]{2,1,0:T(8,128)(2,1)S(1)} %bitcast.20, ...), custom_call_target="tpu_custom_call" | custom-call | flops 2113536 | bytes 3170304 | tf_op jit(solution)/shard_map/ring_step/pallas_call | solution.py:195
  76.8 2.7 %collective-permute-start.11 = (s16[16,16512]{1,0:T(8,128)(2,1)}, s16[16,16512]{1,0:T(8,128)(2,1)S(1)}, u32[]{:S(2)}, u32[]{:S(2)}) collective-permute-start(s16[16,16512]{1,0:T(8,128)(2,1)} %get-tuple-element.26), channel_id=1, source_target_pairs={{2,0},{4,2},{6,4},{8,6},{10,8},{12,10},{14,12},{0,14},{3,1},{5,3},... | collective-permute-start | bytes 1585160 | tf_op jit(solution)/shard_map/ppermute | solution.py:226
  79.5 2.3 %copy-done.4 = s16[8,16,16512]{2,1,0:T(8,128)(2,1)S(1)} copy-done((s16[8,16,16512]{2,1,0:T(8,128)(2,1)S(1)}, s16[8,16,16512]{2,1,0:T(8,128)(2,1)}, u32[]{:S(2)}) %copy-start.4) | copy-done | bytes 4227096
  81.9 1.8 %ring_step.7 = (s16[16,16512]{1,0:T(8,128)(2,1)}, s16[16,16512]{1,0:T(8,128)(2,1)S(1)}) custom-call(s32[2]{0:T(128)S(1)} %pad_add_fusion.1.at, s16[16,16512]{1,0:T(8,128)(2,1)S(1)} %collective-permute-done.2.got_r, s16[16,16512]{1,0:T(8,128)(2,1)S(1)} %collective-permute-done.3.got_l, s16[8,16,16512]{2,1,0:T(8,128)(2,1)S(1)} %copy-done.4, ...), custom_call_target="tpu_custom_call" | custom-call | flops 2113536 | bytes 3170304 | tf_op jit(solution)/shard_map/ring_step/pallas_call | solution.py:195
  83.6 2.7 %collective-permute-start.5 = (s16[16,16512]{1,0:T(8,128)(2,1)S(1)}, s16[16,16512]{1,0:T(8,128)(2,1)S(1)}, u32[]{:S(2)}, u32[]{:S(2)}) collective-permute-start(s16[16,16512]{1,0:T(8,128)(2,1)S(1)} %get-tuple-element.22), channel_id=1, source_target_pairs={{2,0},{4,2},{6,4},{8,6},{10,8},{12,10},{14,12},{0,14},{3,1},{5,3},... | collective-permute-start | bytes 1585160 | tf_op jit(solution)/shard_map/ppermute | solution.py:226
  86.3 3.5 %collective-permute-done.10.got_r = s16[16,16512]{1,0:T(8,128)(2,1)S(1)} collective-permute-done((s16[16,16512]{1,0:T(8,128)(2,1)}, s16[16,16512]{1,0:T(8,128)(2,1)S(1)}, u32[]{:S(2)}, u32[]{:S(2)}) %collective-permute-start.10) | collective-permute-done | bytes 528416 | tf_op jit(solution)/shard_map/ppermute | solution.py:225
  89.8 2.2 %ring_step.10 = (s16[16,16512]{1,0:T(8,128)(2,1)}, s16[16,16512]{1,0:T(8,128)(2,1)}) custom-call(s32[2]{0:T(128)S(1)} %pad_add_fusion.1.at, s16[16,16512]{1,0:T(8,128)(2,1)S(1)} %collective-permute-done.10.got_r, s16[16,16512]{1,0:T(8,128)(2,1)S(1)} %collective-permute-done.11.got_l, s16[8,16,16512]{2,1,0:T(8,128)(2,1)S(1)} %bitcast.22, ...), custom_call_target="tpu_custom_call" | custom-call | flops 2113536 | bytes 3170304 | tf_op jit(solution)/shard_map/ring_step/pallas_call | solution.py:195
  93.0 1.7 %collective-permute-start.13 = (s16[16,16512]{1,0:T(8,128)(2,1)}, s16[16,16512]{1,0:T(8,128)(2,1)S(1)}, u32[]{:S(2)}, u32[]{:S(2)}) collective-permute-start(s16[16,16512]{1,0:T(8,128)(2,1)} %get-tuple-element.28), channel_id=1, source_target_pairs={{2,0},{4,2},{6,4},{8,6},{10,8},{12,10},{14,12},{0,14},{3,1},{5,3},... | collective-permute-start | bytes 1585160 | tf_op jit(solution)/shard_map/ppermute | solution.py:226
  94.8 6.4 %collective-permute-done.4.got_r = s16[16,16512]{1,0:T(8,128)(2,1)S(1)} collective-permute-done((s16[16,16512]{1,0:T(8,128)(2,1)}, s16[16,16512]{1,0:T(8,128)(2,1)S(1)}, u32[]{:S(2)}, u32[]{:S(2)}) %collective-permute-start.4) | collective-permute-done | bytes 528416 | tf_op jit(solution)/shard_map/ppermute | solution.py:225
  101.1 2.2 %copy-done.5 = s16[8,16,16512]{2,1,0:T(8,128)(2,1)S(1)} copy-done((s16[8,16,16512]{2,1,0:T(8,128)(2,1)S(1)}, s16[8,16,16512]{2,1,0:T(8,128)(2,1)}, u32[]{:S(2)}) %copy-start.5) | copy-done | bytes 4227096
  105.8 1.7 %collective-permute-start.7 = (s16[16,16512]{1,0:T(8,128)(2,1)S(1)}, s16[16,16512]{1,0:T(8,128)(2,1)S(1)}, u32[]{:S(2)}, u32[]{:S(2)}) collective-permute-start(s16[16,16512]{1,0:T(8,128)(2,1)S(1)} %get-tuple-element.24), channel_id=1, source_target_pairs={{2,0},{4,2},{6,4},{8,6},{10,8},{12,10},{14,12},{0,14},{3,1},{5,3},... | collective-permute-start | bytes 1585160 | tf_op jit(solution)/shard_map/ppermute | solution.py:226
  107.4 5.0 %collective-permute-done.12.got_r = s16[16,16512]{1,0:T(8,128)(2,1)S(1)} collective-permute-done((s16[16,16512]{1,0:T(8,128)(2,1)}, s16[16,16512]{1,0:T(8,128)(2,1)S(1)}, u32[]{:S(2)}, u32[]{:S(2)}) %collective-permute-start.12) | collective-permute-done | bytes 528416 | tf_op jit(solution)/shard_map/ppermute | solution.py:225
  114.9 1.7 %collective-permute-start.15 = (s16[16,16512]{1,0:T(8,128)(2,1)S(1)}, s16[16,16512]{1,0:T(8,128)(2,1)S(1)}, u32[]{:S(2)}, u32[]{:S(2)}) collective-permute-start(s16[16,16512]{1,0:T(8,128)(2,1)S(1)} %get-tuple-element.30), channel_id=1, source_target_pairs={{2,0},{4,2},{6,4},{8,6},{10,8},{12,10},{14,12},{0,14},{3,1},{5,3},... | collective-permute-start | bytes 1585160 | tf_op jit(solution)/shard_map/ppermute | solution.py:226
  116.6 7.2 %collective-permute-done.6.got_r = s16[16,16512]{1,0:T(8,128)(2,1)S(1)} collective-permute-done((s16[16,16512]{1,0:T(8,128)(2,1)S(1)}, s16[16,16512]{1,0:T(8,128)(2,1)S(1)}, u32[]{:S(2)}, u32[]{:S(2)}) %collective-permute-start.6) | collective-permute-done | bytes 528416 | tf_op jit(solution)/shard_map/ppermute | solution.py:225
  125.3 12.3 %all-to-all-start = ((s16[32,80,128]{2,1,0:T(8,128)(2,1)}), s16[32,80,128]{2,1,0:T(8,128)(2,1)S(1)}, u32[]{:S(2)}, u32[]{:S(2)}) async-start(s16[32,80,128]{2,1,0:T(8,128)(2,1)} %bitcast.10), calls=%async_computation | async-start | bytes 1310720 | tf_op jit(solution)/shard_map/all_to_all | solution.py:399
  137.7 2.2 %copy-done.1 = s16[8,16,16512]{2,1,0:T(8,128)(2,1)S(1)} copy-done((s16[8,16,16512]{2,1,0:T(8,128)(2,1)S(1)}, s16[8,16,16512]{2,1,0:T(8,128)(2,1)}, u32[]{:S(2)}) %copy-start.1) | copy-done | bytes 4227096
  141.0 1.5 collective-permute-start.16
  142.4 10.1 %collective-permute-done.16.got = s16[16,8320]{1,0:T(8,128)(2,1)S(1)} collective-permute-done((s16[16,8320]{1,0:T(8,128)(2,1)S(1)}, s16[16,8320]{1,0:T(8,128)(2,1)S(1)}, u32[]{:S(2)}, u32[]{:S(2)}) %collective-permute-start.16) | collective-permute-done | bytes 266272 | tf_op jit(solution)/shard_map/ppermute | solution.py:401
  (64 shorter events, 13.3 us)
Async XLA Ops:
  0.8 2.4 %copy-start.8 = (bf16[100,100,192]{1,2,0:T(8,128)(2,1)S(1)}, bf16[100,100,192]{1,2,0:T(8,128)(2,1)}, u32[]{:S(2)}) copy-start(bf16[100,100,192]{1,2,0:T(8,128)(2,1)} %param.3) | copy-start | bytes 11520004
  9.9 2.8 %copy-start.6 = (bf16[192,16384]{1,0:T(8,128)(2,1)S(1)}, bf16[192,16384]{1,0:T(8,128)(2,1)}, u32[]{:S(2)}) copy-start(bf16[192,16384]{1,0:T(8,128)(2,1)} %right.3) | copy-start | bytes 18874372
  28.2 23.8 %collective-permute-start = (s16[16,8320]{1,0:T(8,128)(2,1)S(1)}, s16[16,8320]{1,0:T(8,128)(2,1)S(1)}, u32[]{:S(2)}, u32[]{:S(2)}) collective-permute-start(s16[16,8320]{1,0:T(8,128)(2,1)S(1)} %get-tuple-element.36), channel_id=1, source_target_pairs={{0,2},{2,4},{4,6},{6,8},{8,10},{10,12},{12,14},{14,0},{1,3},{3,5},... | collective-permute-start | bytes 798728 | tf_op jit(solution)/shard_map/ppermute | solution.py:225
  30.7 21.3 %collective-permute-start.1 = (s16[16,8320]{1,0:T(8,128)(2,1)S(1)}, s16[16,8320]{1,0:T(8,128)(2,1)S(1)}, u32[]{:S(2)}, u32[]{:S(2)}) collective-permute-start(s16[16,8320]{1,0:T(8,128)(2,1)S(1)} %get-tuple-element.35), channel_id=1, source_target_pairs={{2,0},{4,2},{6,4},{8,6},{10,8},{12,10},{14,12},{0,14},{3,1},{5,3},... | collective-permute-start | bytes 798728 | tf_op jit(solution)/shard_map/ppermute | solution.py:226
  34.7 2.8 %copy-start.7 = (bf16[192,16384]{1,0:T(8,128)(2,1)S(1)}, bf16[192,16384]{1,0:T(8,128)(2,1)}, u32[]{:S(2)}) copy-start(bf16[192,16384]{1,0:T(8,128)(2,1)} %right.3) | copy-start | bytes 18874372
  51.9 22.9 %slice-start = ((s8[4227072]{0:T(1024)(128)(4,1)}), s8[4194304]{0:T(1024)(128)(4,1)S(1)}, s32[]{:S(2)}) async-start(s8[4227072]{0:T(1024)(128)(4,1)} %bitcast.19), calls=%async_computation.1 | async-start | bytes 8388608
  52.0 22.9 %slice-start.1 = ((s8[4227072]{0:T(1024)(128)(4,1)}), s8[32768]{0:T(1024)(128)(4,1)S(1)}, s32[]{:S(2)}) async-start(s8[4227072]{0:T(1024)(128)(4,1)} %bitcast.19), calls=%async_computation.2 | async-start | bytes 65536
  52.0 2.3 %copy-start.3 = (s16[8,16,16512]{2,1,0:T(8,128)(2,1)S(1)}, s16[8,16,16512]{2,1,0:T(8,128)(2,1)}, u32[]{:S(2)}) copy-start(s16[8,16,16512]{2,1,0:T(8,128)(2,1)} %copy-done.2) | copy-start | bytes 12681220
  55.3 24.2 %collective-permute-start.2 = (s16[16,16512]{1,0:T(8,128)(2,1)S(1)}, s16[16,16512]{1,0:T(8,128)(2,1)S(1)}, u32[]{:S(2)}, u32[]{:S(2)}) collective-permute-start(s16[16,16512]{1,0:T(8,128)(2,1)S(1)} %get-tuple-element.19), channel_id=1, source_target_pairs={{0,2},{2,4},{4,6},{6,8},{8,10},{10,12},{12,14},{14,0},{1,3},{3,5},... | collective-permute-start | bytes 1585160 | tf_op jit(solution)/shard_map/ppermute | solution.py:225
  55.4 24.1 %collective-permute-start.3 = (s16[16,16512]{1,0:T(8,128)(2,1)S(1)}, s16[16,16512]{1,0:T(8,128)(2,1)S(1)}, u32[]{:S(2)}, u32[]{:S(2)}) collective-permute-start(s16[16,16512]{1,0:T(8,128)(2,1)S(1)} %get-tuple-element.20), channel_id=1, source_target_pairs={{2,0},{4,2},{6,4},{8,6},{10,8},{12,10},{14,12},{0,14},{3,1},{5,3},... | collective-permute-start | bytes 1585160 | tf_op jit(solution)/shard_map/ppermute | solution.py:226
  58.1 16.7 %collective-permute-start.8 = (s16[16,8320]{1,0:T(8,128)(2,1)S(1)}, s16[16,8320]{1,0:T(8,128)(2,1)S(1)}, u32[]{:S(2)}, u32[]{:S(2)}) collective-permute-start(s16[16,8320]{1,0:T(8,128)(2,1)S(1)} %get-tuple-element.34), channel_id=1, source_target_pairs={{0,2},{2,4},{4,6},{6,8},{8,10},{10,12},{12,14},{14,0},{1,3},{3,5},... | collective-permute-start | bytes 798728 | tf_op jit(solution)/shard_map/ppermute | solution.py:225
  58.2 16.6 %collective-permute-start.9 = (s16[16,8320]{1,0:T(8,128)(2,1)S(1)}, s16[16,8320]{1,0:T(8,128)(2,1)S(1)}, u32[]{:S(2)}, u32[]{:S(2)}) collective-permute-start(s16[16,8320]{1,0:T(8,128)(2,1)S(1)} %get-tuple-element.33), channel_id=1, source_target_pairs={{2,0},{4,2},{6,4},{8,6},{10,8},{12,10},{14,12},{0,14},{3,1},{5,3},... | collective-permute-start | bytes 798728 | tf_op jit(solution)/shard_map/ppermute | solution.py:226
  76.8 13.0 %collective-permute-start.10 = (s16[16,16512]{1,0:T(8,128)(2,1)}, s16[16,16512]{1,0:T(8,128)(2,1)S(1)}, u32[]{:S(2)}, u32[]{:S(2)}) collective-permute-start(s16[16,16512]{1,0:T(8,128)(2,1)} %get-tuple-element.25), channel_id=1, source_target_pairs={{0,2},{2,4},{4,6},{6,8},{8,10},{10,12},{12,14},{14,0},{1,3},{3,5},... | collective-permute-start | bytes 1585160 | tf_op jit(solution)/shard_map/ppermute | solution.py:225
  76.8 13.0 %collective-permute-start.11 = (s16[16,16512]{1,0:T(8,128)(2,1)}, s16[16,16512]{1,0:T(8,128)(2,1)S(1)}, u32[]{:S(2)}, u32[]{:S(2)}) collective-permute-start(s16[16,16512]{1,0:T(8,128)(2,1)} %get-tuple-element.26), channel_id=1, source_target_pairs={{2,0},{4,2},{6,4},{8,6},{10,8},{12,10},{14,12},{0,14},{3,1},{5,3},... | collective-permute-start | bytes 1585160 | tf_op jit(solution)/shard_map/ppermute | solution.py:226
  79.4 10.4 %slice-start.2 = ((s8[4227072]{0:T(1024)(128)(4,1)}), s8[4194304]{0:T(1024)(128)(4,1)S(1)}, s32[]{:S(2)}) async-start(s8[4227072]{0:T(1024)(128)(4,1)} %bitcast.21), calls=%async_computation.3 | async-start | bytes 8388608
  79.5 10.3 %slice-start.3 = ((s8[4227072]{0:T(1024)(128)(4,1)}), s8[32768]{0:T(1024)(128)(4,1)S(1)}, s32[]{:S(2)}) async-start(s8[4227072]{0:T(1024)(128)(4,1)} %bitcast.21), calls=%async_computation.4 | async-start | bytes 65536
  79.5 2.3 %copy-start.4 = (s16[8,16,16512]{2,1,0:T(8,128)(2,1)S(1)}, s16[8,16,16512]{2,1,0:T(8,128)(2,1)}, u32[]{:S(2)}) copy-start(s16[8,16,16512]{2,1,0:T(8,128)(2,1)} %copy-done.2) | copy-start | bytes 12681220
  83.6 17.5 %collective-permute-start.4 = (s16[16,16512]{1,0:T(8,128)(2,1)}, s16[16,16512]{1,0:T(8,128)(2,1)S(1)}, u32[]{:S(2)}, u32[]{:S(2)}) collective-permute-start(s16[16,16512]{1,0:T(8,128)(2,1)} %get-tuple-element.21), channel_id=1, source_target_pairs={{0,2},{2,4},{4,6},{6,8},{8,10},{10,12},{12,14},{14,0},{1,3},{3,5},... | collective-permute-start | bytes 1585160 | tf_op jit(solution)/shard_map/ppermute | solution.py:225
  83.6 17.5 %collective-permute-start.5 = (s16[16,16512]{1,0:T(8,128)(2,1)S(1)}, s16[16,16512]{1,0:T(8,128)(2,1)S(1)}, u32[]{:S(2)}, u32[]{:S(2)}) collective-permute-start(s16[16,16512]{1,0:T(8,128)(2,1)S(1)} %get-tuple-element.22), channel_id=1, source_target_pairs={{2,0},{4,2},{6,4},{8,6},{10,8},{12,10},{14,12},{0,14},{3,1},{5,3},... | collective-permute-start | bytes 1585160 | tf_op jit(solution)/shard_map/ppermute | solution.py:226
  92.0 20.4 %collective-permute-start.12 = (s16[16,16512]{1,0:T(8,128)(2,1)}, s16[16,16512]{1,0:T(8,128)(2,1)S(1)}, u32[]{:S(2)}, u32[]{:S(2)}) collective-permute-start(s16[16,16512]{1,0:T(8,128)(2,1)} %get-tuple-element.27), channel_id=1, source_target_pairs={{0,2},{2,4},{4,6},{6,8},{8,10},{10,12},{12,14},{14,0},{1,3},{3,5},... | collective-permute-start | bytes 1585160 | tf_op jit(solution)/shard_map/ppermute | solution.py:225
  93.0 19.5 %collective-permute-start.13 = (s16[16,16512]{1,0:T(8,128)(2,1)}, s16[16,16512]{1,0:T(8,128)(2,1)S(1)}, u32[]{:S(2)}, u32[]{:S(2)}) collective-permute-start(s16[16,16512]{1,0:T(8,128)(2,1)} %get-tuple-element.28), channel_id=1, source_target_pairs={{2,0},{4,2},{6,4},{8,6},{10,8},{12,10},{14,12},{0,14},{3,1},{5,3},... | collective-permute-start | bytes 1585160 | tf_op jit(solution)/shard_map/ppermute | solution.py:226
  94.7 17.8 %slice-start.4 = ((s8[4227072]{0:T(1024)(128)(4,1)}), s8[4194304]{0:T(1024)(128)(4,1)S(1)}, s32[]{:S(2)}) async-start(s8[4227072]{0:T(1024)(128)(4,1)} %bitcast.23), calls=%async_computation.5 | async-start | bytes 8388608
  94.8 17.7 %slice-start.5 = ((s8[4227072]{0:T(1024)(128)(4,1)}), s8[32768]{0:T(1024)(128)(4,1)S(1)}, s32[]{:S(2)}) async-start(s8[4227072]{0:T(1024)(128)(4,1)} %bitcast.23), calls=%async_computation.6 | async-start | bytes 65536
  104.7 19.1 %collective-permute-start.6 = (s16[16,16512]{1,0:T(8,128)(2,1)S(1)}, s16[16,16512]{1,0:T(8,128)(2,1)S(1)}, u32[]{:S(2)}, u32[]{:S(2)}) collective-permute-start(s16[16,16512]{1,0:T(8,128)(2,1)S(1)} %get-tuple-element.23), channel_id=1, source_target_pairs={{0,2},{2,4},{4,6},{6,8},{8,10},{10,12},{12,14},{14,0},{1,3},{3,5},... | collective-permute-start | bytes 1585160 | tf_op jit(solution)/shard_map/ppermute | solution.py:225
  105.8 18.0 %slice-start.6 = ((s8[4227072]{0:T(1024)(128)(4,1)}), s8[4194304]{0:T(1024)(128)(4,1)S(1)}, s32[]{:S(2)}) async-start(s8[4227072]{0:T(1024)(128)(4,1)} %bitcast.25), calls=%async_computation.7 | async-start | bytes 8388608
  105.8 18.0 %slice-start.7 = ((s8[4227072]{0:T(1024)(128)(4,1)}), s8[32768]{0:T(1024)(128)(4,1)S(1)}, s32[]{:S(2)}) async-start(s8[4227072]{0:T(1024)(128)(4,1)} %bitcast.25), calls=%async_computation.8 | async-start | bytes 65536
  105.8 18.0 %collective-permute-start.7 = (s16[16,16512]{1,0:T(8,128)(2,1)S(1)}, s16[16,16512]{1,0:T(8,128)(2,1)S(1)}, u32[]{:S(2)}, u32[]{:S(2)}) collective-permute-start(s16[16,16512]{1,0:T(8,128)(2,1)S(1)} %get-tuple-element.24), channel_id=1, source_target_pairs={{2,0},{4,2},{6,4},{8,6},{10,8},{12,10},{14,12},{0,14},{3,1},{5,3},... | collective-permute-start | bytes 1585160 | tf_op jit(solution)/shard_map/ppermute | solution.py:226
  113.8 23.9 %collective-permute-start.14 = (s16[16,16512]{1,0:T(8,128)(2,1)S(1)}, s16[16,16512]{1,0:T(8,128)(2,1)S(1)}, u32[]{:S(2)}, u32[]{:S(2)}) collective-permute-start(s16[16,16512]{1,0:T(8,128)(2,1)S(1)} %get-tuple-element.29), channel_id=1, source_target_pairs={{0,2},{2,4},{4,6},{6,8},{8,10},{10,12},{12,14},{14,0},{1,3},{3,5},... | collective-permute-start | bytes 1585160 | tf_op jit(solution)/shard_map/ppermute | solution.py:225
  114.9 22.8 %collective-permute-start.15 = (s16[16,16512]{1,0:T(8,128)(2,1)S(1)}, s16[16,16512]{1,0:T(8,128)(2,1)S(1)}, u32[]{:S(2)}, u32[]{:S(2)}) collective-permute-start(s16[16,16512]{1,0:T(8,128)(2,1)S(1)} %get-tuple-element.30), channel_id=1, source_target_pairs={{2,0},{4,2},{6,4},{8,6},{10,8},{12,10},{14,12},{0,14},{3,1},{5,3},... | collective-permute-start | bytes 1585160 | tf_op jit(solution)/shard_map/ppermute | solution.py:226
  125.3 27.3 %all-to-all-start = ((s16[32,80,128]{2,1,0:T(8,128)(2,1)}), s16[32,80,128]{2,1,0:T(8,128)(2,1)S(1)}, u32[]{:S(2)}, u32[]{:S(2)}) async-start(s16[32,80,128]{2,1,0:T(8,128)(2,1)} %bitcast.10), calls=%async_computation | async-start | bytes 1310720 | tf_op jit(solution)/shard_map/all_to_all | solution.py:399
  137.7 2.2 %copy-start.1 = (s16[8,16,16512]{2,1,0:T(8,128)(2,1)S(1)}, s16[8,16,16512]{2,1,0:T(8,128)(2,1)}, u32[]{:S(2)}) copy-start(s16[8,16,16512]{2,1,0:T(8,128)(2,1)} %copy-done) | copy-start | bytes 12681220
  141.0 11.6 %collective-permute-start.16 = (s16[16,8320]{1,0:T(8,128)(2,1)S(1)}, s16[16,8320]{1,0:T(8,128)(2,1)S(1)}, u32[]{:S(2)}, u32[]{:S(2)}) collective-permute-start(s16[16,8320]{1,0:T(8,128)(2,1)S(1)} %get-tuple-element.32), channel_id=1, source_target_pairs={{0,1},{1,0},{2,3},{3,2},{4,5},{5,4},{6,7},{7,6},{8,9},{9,8},{10,11... | collective-permute-start | bytes 798728 | tf_op jit(solution)/shard_map/ppermute | solution.py:401
  (3 other events, 6.2 us)

commit v2 on v1

v2 whole, which is shorter than its diff:
```python
import functools

import jax
import jax.numpy as jnp
from jax import lax
from jax.experimental import pallas as pl
from jax.experimental.pallas import tpu as pltpu
from jax.sharding import Mesh
from jax.sharding import PartitionSpec as P

OB = 2
PB = OB * OB
A_DEV = 32
AW = 512
F32, I16 = jnp.float32, jnp.int16
ROW, Z, XL = "row", "z", "xl"
LANES = 128
TILES = A_DEV * AW // (16 * LANES)
ROW_W = TILES * LANES
PITCH = A_DEV + 1
PARTS = 1
TOP = 32700.0
STEPS = 256.0


def params(mib=32):
    return pltpu.CompilerParams(vmem_limit_bytes=mib << 20)


def cost(flops, bytes_accessed):
    return pl.CostEstimate(flops=flops, bytes_accessed=bytes_accessed, transcendentals=0)


def hbm():
    return pl.BlockSpec(memory_space=pltpu.HBM)


def vmem():
    return pl.BlockSpec(memory_space=pltpu.VMEM)


def scale_of(tiles):
    most = functools.reduce(jnp.maximum, [jnp.abs(t) for t in tiles])
    most = jnp.max(most, axis=0, keepdims=True)
    code = jnp.ceil(jnp.log2(jnp.maximum(most, 2.0**-100)) * STEPS)
    return code, TOP * jnp.exp2(code * (-1.0 / STEPS))


def coded(x, factor):
    return jnp.round(x * factor).astype(jnp.int32).astype(I16)


def factors(codes):
    return jnp.exp2(codes.astype(F32) * (1.0 / STEPS)) * (1.0 / TOP)


def column(k, n):
    return k * ROW_W + (LANES if k >= n // 2 else 0)


def get_row(ref, start, factor):
    return [
        ref[:, start + t * LANES : start + (t + 1) * LANES].astype(jnp.int32).astype(F32) * factor
        for t in range(TILES)
    ]


def put_row(ref, start, tiles):
    code, factor = scale_of(tiles)
    for t, tile in enumerate(tiles):
        ref[:, start + t * LANES : start + (t + 1) * LANES] = coded(tile, factor)
    return code


def scale_tile(codes):
    rows = codes + [jnp.zeros((1, LANES), F32)] * (16 - len(codes))
    return jnp.concatenate(rows, axis=0).astype(jnp.int32).astype(I16)


UNROLL = 4


def gather_kernel(blocks, pages, out, picked):
    depth, orbitals = pages.shape[1], pages.shape[2]
    pairs = blocks.shape[1]
    lane = lax.broadcasted_iota(jnp.int32, (depth, LANES), 1)
    blank = jnp.zeros((depth, LANES - orbitals), F32)
    picked[...] = jnp.zeros_like(picked)

    def turned(page, shift):
        whole = jnp.concatenate([pages[page].astype(F32), blank], axis=1)
        return pltpu.roll(whole, lax.rem(shift + LANES, LANES), 1)

    def some(step, _):
        forward, mirrored = picked[0], picked[1]
        for i in range(UNROLL):
            pair = step * UNROLL + i
            first, second = blocks[0, pair] * OB, blocks[1, pair] * OB
            for s in range(OB):
                to = pair * PB + s * OB
                here = (lane >= to) & (lane < to + OB)
                forward = jnp.where(here, turned(first + s, to - second), forward)
                mirrored = jnp.where(here, turned(second + s, to - first), mirrored)
        picked[0] = forward
        picked[1] = mirrored
        return 0

    lax.fori_loop(0, pairs // UNROLL, some, 0)
    mirrored = picked[1]
    which = lax.rem(lane, PB)
    mirrored = jnp.where(
        which == 1, pltpu.roll(mirrored, LANES - 1, 1), jnp.where(which == 2, pltpu.roll(mirrored, 1, 1), mirrored)
    )
    out[:LANES] = mirrored.T.astype(out.dtype)
    out[LANES:] = picked[0].T.astype(out.dtype)


def gather(amplitudes, blocks):
    depth = amplitudes.shape[2]
    rows = blocks.shape[0] * PB
    return pl.pallas_call(
        gather_kernel,
        out_shape=jax.ShapeDtypeStruct((2 * rows, depth), jnp.bfloat16),
        in_specs=[pl.BlockSpec(memory_space=pltpu.SMEM), vmem()],
        out_specs=vmem(),
        scratch_shapes=[pltpu.VMEM((2, depth, LANES), F32)],
        compiler_params=params(24),
        name="pick_rows",
    )(blocks.T, jnp.swapaxes(amplitudes, 1, 2))


GRID = 8


def fill(left, right, whole):
    step = pl.program_id(0)
    rows = left.shape[0]
    each = A_DEV // GRID
    for i in range(each):
        part = jnp.dot(left[...], right[:, i * AW : (i + 1) * AW], preferred_element_type=F32)
        for c in range(AW // LANES):
            whole[c, pl.ds(step * each + i, rows, stride=PITCH), :] = part[:, c * LANES : (c + 1) * LANES]


def filled(whole, row):
    return [
        whole[c, pl.ds(row * PITCH + h * 16, 16), :] for h in range(2) for c in range(AW // LANES)
    ]


def product_kernel(z_n, n, at, left, right, *refs):
    *outs, out_r, out_l, whole, coded_rows, sems = refs
    fill(left, right, whole)

    @pl.when(pl.program_id(0) == GRID - 1)
    def _():
        middle = n // 2 * ROW_W
        for kind in range(2):
            out = outs[kind]
            base = kind * z_n

            def one(z, _):
                spot = coded_rows.at[base + z]
                codes = [put_row(spot, column(k, n), filled(whole, (base + z) * n + k)) for k in range(n)]
                spot[:, middle : middle + LANES] = scale_tile(codes)
                pltpu.make_async_copy(spot, out.at[z], sems.at[base + z]).start()
                return 0

            lax.fori_loop(0, z_n, one, 0)
            opposite = coded_rows.at[base + at[0]]
            out_r[kind] = opposite[:, : middle + LANES]
            out_l[kind] = opposite[:, middle:]
        for kind in range(2):
            for z in range(z_n):
                spot = kind * z_n + z
                pltpu.make_async_copy(coded_rows.at[spot], outs[kind].at[z], sems.at[spot]).wait()


def product(left, integrals, z_n):
    depth, width = integrals.shape
    rows = left.shape[0]
    n = rows // 2 // z_n
    total = n * ROW_W + LANES
    half = n // 2 * ROW_W + LANES
    at = lax.rem(lax.axis_index(Z) + z_n // 2, z_n)[None]
    end = jax.ShapeDtypeStruct((2, 16, half), I16)
    end_spec = pl.BlockSpec((2, 16, half), lambda s: (0, 0, 0))
    *parts, r, l = pl.pallas_call(
        functools.partial(product_kernel, z_n, n),
        grid=(GRID,),
        out_shape=(pltpu.HBM((z_n, 16, total), I16),) * 2 + (end, end),
        in_specs=[
            smem(),
            pl.BlockSpec((rows, depth), lambda s: (0, 0)),
            pl.BlockSpec((depth, width // GRID), lambda s: (0, s)),
        ],
        out_specs=[hbm(), hbm(), end_spec, end_spec],
        scratch_shapes=[
            pltpu.VMEM(matrices(rows), F32),
            pltpu.VMEM((2 * z_n, 16, total), I16),
            pltpu.SemaphoreType.DMA((2 * z_n,)),
        ],
        compiler_params=params(PRODUCT_MIB),
        cost_estimate=cost(2 * rows * depth * width, 2 * depth * width + 2 * rows * width),
        name="product",
    )(at, left, in_hbm(integrals))
    return parts, r, l


def in_hbm(x):
    return pltpu.with_memory_space_constraint(x, pltpu.HBM)


PRODUCT_MIB = 48


def matrices(rows):
    return (AW // LANES, rows * PITCH, LANES)


def step_kernel(n, kind, first, at, got_r, got_l, parts, after, out_r, out_l, own_r, own_l, sems):
    half = n // 2
    middle = half * ROW_W
    if first:
        got_r, got_l = got_r.at[kind], got_l.at[kind]
    copies = [
        pltpu.make_async_copy(parts.at[at[i]], own, sems.at[i]) for i, own in enumerate((own_r, own_l))
    ]
    for copy in copies:
        copy.start()
    for side, got, own, out in ((0, got_r, own_r, out_r), (1, got_l, own_l, out_l)):
        copies[side].wait()
        own_codes = own[:, middle : middle + LANES].astype(jnp.int32).astype(F32)
        own_f = factors(own_codes)
        if first:
            spot = middle if side == 0 else 0
            got_f = factors(got[:, spot : spot + LANES].astype(jnp.int32))
        else:
            got_f = factors(got[:, middle : middle + LANES].astype(jnp.int32))
        codes = []
        for k in range(n):
            start = column(k, n)
            if first and (k < half) != (side == 0):
                out[:, start : start + ROW_W] = own[:, start : start + ROW_W]
                codes.append(own_codes[k : k + 1])
                continue
            came = start - (middle if first and side == 1 else 0)
            a = get_row(got, came, got_f[k : k + 1])
            b = get_row(own, start, own_f[k : k + 1])
            codes.append(put_row(out, start, [x + y for x, y in zip(a, b)]))
        out[:, middle : middle + LANES] = scale_tile(codes)


def smem():
    return pl.BlockSpec(memory_space=pltpu.SMEM)


def anywhere():
    return pl.BlockSpec(memory_space=pl.ANY)


def ring_step(got_r, got_l, parts, at, n, kind, first, after):
    width = parts.shape[2]
    shape = jax.ShapeDtypeStruct((16, width), I16)
    return pl.pallas_call(
        functools.partial(step_kernel, n, kind, first),
        out_shape=(shape, shape),
        in_specs=[smem(), vmem(), vmem(), hbm(), anywhere()],
        out_specs=[vmem(), vmem()],
        scratch_shapes=[pltpu.VMEM((16, width), I16), pltpu.VMEM((16, width), I16), pltpu.SemaphoreType.DMA((2,))],
        compiler_params=params(16),
        cost_estimate=cost(16 * width * 8, 16 * width * 12),
        name="ring_step",
    )(at, got_r, got_l, in_hbm(parts), after)


def rings(streams, r, l, n, z_n):
    me = lax.axis_index(Z)
    right = [(i, (i + 1) % z_n) for i in range(z_n)]
    left = [((i + 1) % z_n, i) for i in range(z_n)]
    far = z_n // 2
    sums = [(lax.ppermute(r, Z, right), lax.ppermute(l, Z, left))] * len(streams)
    for d in range(far - 1, 0, -1):
        at = jnp.stack([lax.rem(me + d, z_n), lax.rem(me + z_n - d, z_n)])
        after = at
        for i, (parts, (r, l)) in enumerate(zip(streams, sums)):
            sums[i] = ring_step(r, l, parts, at, n, i, d == far - 1, after)
            after = sums[i][0]
        sums = [(lax.ppermute(r, Z, right), lax.ppermute(l, Z, left)) for r, l in sums]
    return sums


def end_rows(n, refs):
    middle = n // 2 * ROW_W
    f = [factors(ref[:, middle : middle + LANES].astype(jnp.int32)) for ref in refs]

    def row(k):
        rows = [get_row(ref, column(k, n), g[k : k + 1]) for ref, g in zip(refs, f)]
        return [x + y + w for x, y, w in zip(*rows)]

    return row


def matrix(tiles):
    per = len(tiles) // 2
    return jnp.concatenate(
        [jnp.concatenate(tiles[:per], axis=1), jnp.concatenate(tiles[per:], axis=1)], axis=0
    )


def fetch(parts, at, own, sem):
    copy = pltpu.make_async_copy(parts.at[at], own, sem)
    copy.start()
    copy.wait()


def turn_kernel(n, rows_n, at, got_r, got_l, parts, out, own, sem):
    fetch(parts, at[0], own, sem)
    row = end_rows(n, [got_r, got_l, own])
    groups = n // (2 * PB)
    for xl in range(2):
        codes = []
        for g in range(groups):
            stack = jnp.concatenate([matrix(row((xl * groups + g) * PB + i)) for i in range(PB)], axis=0)
            turned = stack.T
            code, factor = scale_of([turned])
            codes.append(code)
            for to in range(rows_n):
                out[to, xl, g * A_DEV : (g + 1) * A_DEV, :] = coded(turned[to * A_DEV : (to + 1) * A_DEV], factor)
        tile = scale_tile(codes)
        for to in range(rows_n):
            out[to, xl, groups * A_DEV : groups * A_DEV + 16, :] = tile


def turn(got_r, got_l, parts, n, rows_n):
    width = parts.shape[2]
    shape = (rows_n, 2, n // (2 * PB) * A_DEV + 16, LANES)
    return pl.pallas_call(
        functools.partial(turn_kernel, n, rows_n),
        out_shape=jax.ShapeDtypeStruct(shape, I16),
        in_specs=[smem(), vmem(), vmem(), hbm()],
        out_specs=vmem(),
        scratch_shapes=[pltpu.VMEM((16, width), I16), pltpu.SemaphoreType.DMA],
        compiler_params=params(32),
        cost_estimate=cost(16 * width * 8, 16 * width * 8),
        name="turn",
    )(lax.axis_index(Z)[None], got_r, got_l, in_hbm(parts))


def share_kernel(n, at, got_r, got_l, parts, keep, give, own, sem):
    fetch(parts, at[0], own, sem)
    row = end_rows(n, [got_r, got_l, own])
    half = n // 2
    first = at[1] == 0
    codes = []
    for i in range(half):
        low, high = row(i), row(half + i)
        keep[i] = matrix([jnp.where(first, a, b) for a, b in zip(low, high)])
        codes.append(put_row(give, column(i, half), [jnp.where(first, b, a) for a, b in zip(low, high)]))
    give[:, column(half // 2, half) - LANES : column(half // 2, half)] = scale_tile(codes)


def share(got_r, got_l, parts, n):
    width = parts.shape[2]
    half = n // 2
    return pl.pallas_call(
        functools.partial(share_kernel, n),
        out_shape=(
            jax.ShapeDtypeStruct((half, A_DEV, AW), F32),
            jax.ShapeDtypeStruct((16, half * ROW_W + LANES), I16),
        ),
        in_specs=[smem(), vmem(), vmem(), hbm()],
        out_specs=[vmem(), vmem()],
        scratch_shapes=[pltpu.VMEM((16, width), I16), pltpu.SemaphoreType.DMA],
        compiler_params=params(16),
        cost_estimate=cost(16 * width * 8, 16 * width * 8),
        name="share",
    )(jnp.stack([lax.axis_index(Z), lax.axis_index(XL)]), got_r, got_l, in_hbm(parts))


def regroup(tiles):
    count = len(tiles)
    group = LANES // count
    lane = lax.broadcasted_iota(jnp.int32, tiles[0].shape, 1) // group
    out = []
    for k in range(count):
        merged = tiles[k]
        for r in range(count):
            if r != k:
                merged = jnp.where(lane == r, pltpu.roll(tiles[r], (r - k) % count * group, 1), merged)
        out.append(merged)
    return out


def last_kernel(n, rows_n, mirrored, keep_0, got_0, out, total):
    half = n // 2
    groups = half // PB
    at = groups * A_DEV
    f = [[factors(mirrored[r, s, at : at + 16, :].astype(jnp.int32)) for s in range(2)] for r in range(rows_n)]
    middle = half // 2 * ROW_W
    for g in range(groups):
        pieces = []
        for r in range(rows_n):
            both = [
                mirrored[r, s, g * A_DEV : (g + 1) * A_DEV, :].astype(jnp.int32).astype(F32) * f[r][s][g : g + 1]
                for s in range(2)
            ]
            pieces.append(both[0] + both[1])
        per = LANES // A_DEV
        for c in range(rows_n // per):
            for i, tile in enumerate(regroup(pieces[c * per : (c + 1) * per])):
                total[c, pl.ds((g * PB + i) * PITCH, A_DEV), :] = tile
    for part, keep, got in ((0, keep_0, got_0),):
        got_f = factors(got[:, middle : middle + LANES].astype(jnp.int32))
        for k in range(half):
            tiles = get_row(got, column(k, half), got_f[k : k + 1])
            for h in range(2):
                for c in range(AW // LANES):
                    lanes = slice(c * LANES, (c + 1) * LANES)
                    spot = pl.ds((part * half + k) * PITCH + h * 16, 16)
                    tile = tiles[h * (AW // LANES) + c] + keep[k, h * 16 : (h + 1) * 16, lanes]
                    total[c, spot, :] = tile + total[c, spot, :] if part == 0 else tile
    for a in range(A_DEV):
        for c in range(AW // LANES):
            start = a * AW + c * LANES
            out[:, start : start + LANES] = total[c, pl.ds(a, PARTS * half, stride=PITCH), :].astype(out.dtype)


def last(mirrored, shares, n):
    rows = PARTS * n // 2
    rows_n = mirrored.shape[0]
    return pl.pallas_call(
        functools.partial(last_kernel, n, rows_n),
        out_shape=jax.ShapeDtypeStruct((rows, A_DEV * AW), jnp.bfloat16),
        in_specs=[vmem()] * 3,
        out_specs=vmem(),
        scratch_shapes=[pltpu.VMEM(matrices(rows), F32)],
        compiler_params=params(16),
        name="last",
    )(mirrored, *shares)


def swap(keep, give):
    return keep, lax.ppermute(give, XL, [(0, 1), (1, 0)])


def on_device(rows_n, z_n, amplitudes, integrals, blocks):
    picked = gather(amplitudes, blocks)
    rows = picked.shape[0] // 2
    n = rows // z_n
    streams, r, l = product(picked, integrals, z_n)
    (m_r, m_l), (f_r, f_l) = rings(streams, r, l, n, z_n)
    pieces = turn(m_r, m_l, streams[0], n, rows_n)
    shape = pieces.shape
    pieces = pieces.reshape((rows_n * 2,) + shape[2:])
    pieces = lax.all_to_all(pieces, (ROW, XL), 0, 0, tiled=True).reshape(shape)
    keep, got = swap(*share(f_r, f_l, streams[1], n))
    return last(pieces, (keep, got), n)


def solution(mesh):
    rows_n, cols_n = mesh.devices.shape
    finer = Mesh(mesh.devices.reshape(rows_n, cols_n // 2, 2), (ROW, Z, XL))
    return jax.shard_map(
        functools.partial(on_device, rows_n, cols_n // 2),
        mesh=finer,
        in_specs=(P(None, None, (Z, XL)), P((Z, XL), ROW), P()),
        out_specs=P((Z, XL), ROW),
        check_vma=False,
    )
```

time: 154 us -> 127 us (0.82)
  local copies, waits for them, and re-layouts: 23 us -> 3.07 us
  Pallas kernels: 44.9 us -> 36.8 us
  waiting for transfers between devices: 46.2 us -> 51 us
  starting transfers between devices: 39.4 us -> 35.6 us
    unnamed x35 -> x4, local copies, waits for them, and re-layouts: 21.8 us -> 3.07 us
    pallas_call x2 -> x1, Pallas kernels: 24.6 us -> 10.7 us  [product(): pl.pallas_call(functools.partial(product_kernel, z_n, n), grid=(GRID,), o...]
    ppermute x17 -> x15, waiting for transfers between devices: 46.2 us -> 51 us  [the longest x7 39.7 us: rings(): lax.ppermute(r, Z, right)]
    pallas_call x7, Pallas kernels: 16.3 us -> 20.2 us  [the longest x6 17.2 us: ring_step(): pl.pallas_call(functools.partial(step_kernel, n, kind, first), out_shape=...]
    ppermute x17 -> x15, starting transfers between devices: 27.1 us -> 24.6 us  [the longest x7 16.5 us: rings(): lax.ppermute(l, Z, left)]
  transfers between devices with their start and end apart: 18 -> 16, of which waited for: 6 -> 7; matrix products, arithmetic and copies ran while one was open for 0% -> 0% of each run, Pallas kernels for 15% -> 15%
where the time goes in v2:
time: 127 us
  waiting for transfers between devices  51 us (40%)
  Pallas kernels  36.8 us (29%)
  starting transfers between devices  35.6 us (28%)
  local copies, waits for them, and re-layouts  3.07 us (2%)
    ppermute x7, waiting for transfers between devices, rings(): lax.ppermute(r, Z, right)  39.7 us
    pallas_call x6, Pallas kernels, ring_step(): pl.pallas_call(functools.partial(step_kernel, n, kind, first), out_shape=...  17.2 us
    ppermute x7, starting transfers between devices, rings(): lax.ppermute(l, Z, left)  16.5 us
    ppermute x1, waiting for transfers between devices, swap(): return (keep, lax.ppermute(give, XL, [(0, 1), (1, 0)]))  11.3 us
    all_to_all x1, starting transfers between devices, on_device(): pieces = lax.all_to_all(pieces, (ROW, XL), 0, 0, tiled=True).reshape(shape)  11 us
    pallas_call x1, Pallas kernels, product(): pl.pallas_call(functools.partial(product_kernel, z_n, n), grid=(GRID,), o...  10.7 us
    ppermute x7, starting transfers between devices, rings(): lax.ppermute(r, Z, right)  6.62 us
    unnamed x4, local copies, waits for them, and re-layouts  3.07 us
  transfers between devices with their start and end apart: 16, of which 7 were waited for; matrix products, arithmetic and copies ran while one was open for 0% of the time, Pallas kernels for 15%

profile of v2, /device:TPU:1, one launch (start us, length us, event | category | flops | bytes accessed | tf_op | source)
XLA Modules:
  0.0 126.9 jit_solution(16200798774707658619)
XLA Ops:
  0.0 2.4 %copy-done = bf16[100,100,192]{1,2,0:T(8,128)(2,1)S(1)} copy-done((bf16[100,100,192]{1,2,0:T(8,128)(2,1)S(1)}, bf16[100,100,192]{1,2,0:T(8,128)(2,1)}, u32[]{:S(2)}) %copy-start) | copy-done | bytes 3840024
  3.1 3.1 %pick_rows.1.left = bf16[256,192]{1,0:T(8,128)(2,1)S(1)} custom-call(s32[2,32]{1,0:T(2,128)S(1)} %bitcast.15, bf16[100,192,100]{2,1,0:T(8,128)(2,1)S(1)} %bitcast.13), custom_call_target="tpu_custom_call" | custom-call | tf_op jit(solution)/shard_map/pick_rows/pallas_call | solution.py:121
  6.1 10.7 %product.1 = (s16[8,16,16512]{2,1,0:T(8,128)(2,1)}, s16[8,16,16512]{2,1,0:T(8,128)(2,1)}, s16[2,16,8320]{2,1,0:T(8,128)(2,1)S(1)}, s16[2,16,8320]{2,1,0:T(8,128)(2,1)S(1)}) custom-call(s32[1]{0:T(128)} %bitcast.7.at, bf16[256,192]{1,0:T(8,128)(2,1)S(1)} %pick_rows.1.left, bf16[192,16384]{1,0:T(8,128)(2,1)} %right.1), custom_call_target="tpu_custom_call" | custom-call | flops 1610612736 | bytes 14680064 | tf_op jit(solution)/shard_map/product/pallas_call | solution.py:188
  16.8 2.5 %collective-permute-start = (s16[2,16,8320]{2,1,0:T(8,128)(2,1)S(1)}, s16[2,16,8320]{2,1,0:T(8,128)(2,1)S(1)}, u32[]{:S(2)}, u32[]{:S(2)}) collective-permute-start(s16[2,16,8320]{2,1,0:T(8,128)(2,1)S(1)} %get-tuple-element.23), channel_id=1, source_target_pairs={{0,2},{2,4},{4,6},{6,8},{8,10},{10,12},{12,14},{14,0},{1,3},{3,5},... | collective-permute-start | bytes 1597448 | tf_op jit(solution)/shard_map/ppermute | solution.py:282
  19.4 4.0 %collective-permute-start.1 = (s16[2,16,8320]{2,1,0:T(8,128)(2,1)S(1)}, s16[2,16,8320]{2,1,0:T(8,128)(2,1)S(1)}, u32[]{:S(2)}, u32[]{:S(2)}) collective-permute-start(s16[2,16,8320]{2,1,0:T(8,128)(2,1)S(1)} %get-tuple-element.24), channel_id=1, source_target_pairs={{2,0},{4,2},{6,4},{8,6},{10,8},{12,10},{14,12},{0,14},{3,1},{5,3},... | collective-permute-start | bytes 1597448 | tf_op jit(solution)/shard_map/ppermute | solution.py:282
  23.5 11.7 %collective-permute-done.got_r = s16[2,16,8320]{2,1,0:T(8,128)(2,1)S(1)} collective-permute-done((s16[2,16,8320]{2,1,0:T(8,128)(2,1)S(1)}, s16[2,16,8320]{2,1,0:T(8,128)(2,1)S(1)}, u32[]{:S(2)}, u32[]{:S(2)}) %collective-permute-start) | collective-permute-done | bytes 532512 | tf_op jit(solution)/shard_map/ppermute | solution.py:282
  35.2 2.9 %ring_step.6 = (s16[16,16512]{1,0:T(8,128)(2,1)}, s16[16,16512]{1,0:T(8,128)(2,1)}) custom-call(s32[2]{0:T(128)S(1)} %pad_add_fusion.2.at.after, s16[2,16,8320]{2,1,0:T(8,128)(2,1)S(1)} %collective-permute-done.got_r, s16[2,16,8320]{2,1,0:T(8,128)(2,1)S(1)} %collective-permute-done.1.got_l, s16[8,16,16512]{2,1,0:T(8,128)(2,1)} %get-tuple-element.25.parts, ...), custom_call_target="tpu_custom_call" | custom-call | flops 2113536 | bytes 3170304 | tf_op jit(solution)/shard_map/ring_step/pallas_call | solution.py:265
  38.1 2.7 %collective-permute-start.3 = (s16[16,16512]{1,0:T(8,128)(2,1)}, s16[16,16512]{1,0:T(8,128)(2,1)S(1)}, u32[]{:S(2)}, u32[]{:S(2)}) collective-permute-start(s16[16,16512]{1,0:T(8,128)(2,1)} %get-tuple-element.27), channel_id=1, source_target_pairs={{2,0},{4,2},{6,4},{8,6},{10,8},{12,10},{14,12},{0,14},{3,1},{5,3},... | collective-permute-start | bytes 1585160 | tf_op jit(solution)/shard_map/ppermute | solution.py:289
  40.8 2.9 %ring_step.9 = (s16[16,16512]{1,0:T(8,128)(2,1)}, s16[16,16512]{1,0:T(8,128)(2,1)}) custom-call(s32[2]{0:T(128)S(1)} %pad_add_fusion.2.at.after, s16[2,16,8320]{2,1,0:T(8,128)(2,1)S(1)} %collective-permute-done.got_r, s16[2,16,8320]{2,1,0:T(8,128)(2,1)S(1)} %collective-permute-done.1.got_l, s16[8,16,16512]{2,1,0:T(8,128)(2,1)} %get-tuple-element.32.parts, ...), custom_call_target="tpu_custom_call" | custom-call | flops 2113536 | bytes 3170304 | tf_op jit(solution)/shard_map/ring_step/pallas_call | solution.py:265
  43.8 2.7 %collective-permute-start.9 = (s16[16,16512]{1,0:T(8,128)(2,1)}, s16[16,16512]{1,0:T(8,128)(2,1)S(1)}, u32[]{:S(2)}, u32[]{:S(2)}) collective-permute-start(s16[16,16512]{1,0:T(8,128)(2,1)} %get-tuple-element.34), channel_id=1, source_target_pairs={{2,0},{4,2},{6,4},{8,6},{10,8},{12,10},{14,12},{0,14},{3,1},{5,3},... | collective-permute-start | bytes 1585160 | tf_op jit(solution)/shard_map/ppermute | solution.py:289
  46.5 5.3 %collective-permute-done.2.got_r = s16[16,16512]{1,0:T(8,128)(2,1)S(1)} collective-permute-done((s16[16,16512]{1,0:T(8,128)(2,1)}, s16[16,16512]{1,0:T(8,128)(2,1)S(1)}, u32[]{:S(2)}, u32[]{:S(2)}) %collective-permute-start.2) | collective-permute-done | bytes 528416 | tf_op jit(solution)/shard_map/ppermute | solution.py:289
  51.8 3.2 %ring_step.7 = (s16[16,16512]{1,0:T(8,128)(2,1)S(1)}, s16[16,16512]{1,0:T(8,128)(2,1)}) custom-call(s32[2]{0:T(128)S(1)} %pad_add_fusion.1.at.after, s16[16,16512]{1,0:T(8,128)(2,1)S(1)} %collective-permute-done.2.got_r, s16[16,16512]{1,0:T(8,128)(2,1)S(1)} %collective-permute-done.3.got_l, s16[8,16,16512]{2,1,0:T(8,128)(2,1)} %get-tuple-element.25.parts, ...), custom_call_target="tpu_custom_call" | custom-call | flops 2113536 | bytes 3170304 | tf_op jit(solution)/shard_map/ring_step/pallas_call | solution.py:265
  55.1 1.0 collective-permute-start.4
  56.0 1.8 %collective-permute-start.5 = (s16[16,16512]{1,0:T(8,128)(2,1)}, s16[16,16512]{1,0:T(8,128)(2,1)S(1)}, u32[]{:S(2)}, u32[]{:S(2)}) collective-permute-start(s16[16,16512]{1,0:T(8,128)(2,1)} %get-tuple-element.29), channel_id=1, source_target_pairs={{2,0},{4,2},{6,4},{8,6},{10,8},{12,10},{14,12},{0,14},{3,1},{5,3},... | collective-permute-start | bytes 1585160 | tf_op jit(solution)/shard_map/ppermute | solution.py:289
  57.8 5.3 %collective-permute-done.8.got_r = s16[16,16512]{1,0:T(8,128)(2,1)S(1)} collective-permute-done((s16[16,16512]{1,0:T(8,128)(2,1)}, s16[16,16512]{1,0:T(8,128)(2,1)S(1)}, u32[]{:S(2)}, u32[]{:S(2)}) %collective-permute-start.8) | collective-permute-done | bytes 528416 | tf_op jit(solution)/shard_map/ppermute | solution.py:289
  63.1 2.9 %ring_step.10 = (s16[16,16512]{1,0:T(8,128)(2,1)}, s16[16,16512]{1,0:T(8,128)(2,1)S(1)}) custom-call(s32[2]{0:T(128)S(1)} %pad_add_fusion.1.at.after, s16[16,16512]{1,0:T(8,128)(2,1)S(1)} %collective-permute-done.8.got_r, s16[16,16512]{1,0:T(8,128)(2,1)S(1)} %collective-permute-done.9.got_l, s16[8,16,16512]{2,1,0:T(8,128)(2,1)} %get-tuple-element.32.parts, ...), custom_call_target="tpu_custom_call" | custom-call | flops 2113536 | bytes 3170304 | tf_op jit(solution)/shard_map/ring_step/pallas_call | solution.py:265
  66.1 1.0 collective-permute-start.10
  67.0 1.8 %collective-permute-start.11 = (s16[16,16512]{1,0:T(8,128)(2,1)S(1)}, s16[16,16512]{1,0:T(8,128)(2,1)S(1)}, u32[]{:S(2)}, u32[]{:S(2)}) collective-permute-start(s16[16,16512]{1,0:T(8,128)(2,1)S(1)} %get-tuple-element.36), channel_id=1, source_target_pairs={{2,0},{4,2},{6,4},{8,6},{10,8},{12,10},{14,12},{0,14},{3,1},{5,3},... | collective-permute-start | bytes 1585160 | tf_op jit(solution)/shard_map/ppermute | solution.py:289
  68.9 5.6 %collective-permute-done.4.got_r = s16[16,16512]{1,0:T(8,128)(2,1)S(1)} collective-permute-done((s16[16,16512]{1,0:T(8,128)(2,1)S(1)}, s16[16,16512]{1,0:T(8,128)(2,1)S(1)}, u32[]{:S(2)}, u32[]{:S(2)}) %collective-permute-start.4) | collective-permute-done | bytes 528416 | tf_op jit(solution)/shard_map/ppermute | solution.py:289
  74.5 2.4 %ring_step.8 = (s16[16,16512]{1,0:T(8,128)(2,1)S(1)}, s16[16,16512]{1,0:T(8,128)(2,1)S(1)}) custom-call(s32[2]{0:T(128)S(1)} %pad_add_fusion.at.after, s16[16,16512]{1,0:T(8,128)(2,1)S(1)} %collective-permute-done.4.got_r, s16[16,16512]{1,0:T(8,128)(2,1)S(1)} %collective-permute-done.5.got_l, s16[8,16,16512]{2,1,0:T(8,128)(2,1)} %get-tuple-element.25.parts, ...), custom_call_target="tpu_custom_call" | custom-call | flops 2113536 | bytes 3170304 | tf_op jit(solution)/shard_map/ring_step/pallas_call | solution.py:265
  76.9 1.0 collective-permute-start.6
  77.9 1.8 %collective-permute-start.7 = (s16[16,16512]{1,0:T(8,128)(2,1)S(1)}, s16[16,16512]{1,0:T(8,128)(2,1)S(1)}, u32[]{:S(2)}, u32[]{:S(2)}) collective-permute-start(s16[16,16512]{1,0:T(8,128)(2,1)S(1)} %get-tuple-element.31), channel_id=1, source_target_pairs={{2,0},{4,2},{6,4},{8,6},{10,8},{12,10},{14,12},{0,14},{3,1},{5,3},... | collective-permute-start | bytes 1585160 | tf_op jit(solution)/shard_map/ppermute | solution.py:289
  79.7 6.1 %collective-permute-done.10.got_r = s16[16,16512]{1,0:T(8,128)(2,1)S(1)} collective-permute-done((s16[16,16512]{1,0:T(8,128)(2,1)}, s16[16,16512]{1,0:T(8,128)(2,1)S(1)}, u32[]{:S(2)}, u32[]{:S(2)}) %collective-permute-start.10) | collective-permute-done | bytes 528416 | tf_op jit(solution)/shard_map/ppermute | solution.py:289
  85.8 2.8 %ring_step.11 = (s16[16,16512]{1,0:T(8,128)(2,1)}, s16[16,16512]{1,0:T(8,128)(2,1)S(1)}) custom-call(s32[2]{0:T(128)S(1)} %pad_add_fusion.at.after, s16[16,16512]{1,0:T(8,128)(2,1)S(1)} %collective-permute-done.10.got_r, s16[16,16512]{1,0:T(8,128)(2,1)S(1)} %collective-permute-done.11.got_l, s16[8,16,16512]{2,1,0:T(8,128)(2,1)} %get-tuple-element.32.parts, ...), custom_call_target="tpu_custom_call" | custom-call | flops 2113536 | bytes 3170304 | tf_op jit(solution)/shard_map/ring_step/pallas_call | solution.py:265
  89.6 1.8 %collective-permute-start.13 = (s16[16,16512]{1,0:T(8,128)(2,1)S(1)}, s16[16,16512]{1,0:T(8,128)(2,1)S(1)}, u32[]{:S(2)}, u32[]{:S(2)}) collective-permute-start(s16[16,16512]{1,0:T(8,128)(2,1)S(1)} %get-tuple-element.38), channel_id=1, source_target_pairs={{2,0},{4,2},{6,4},{8,6},{10,8},{12,10},{14,12},{0,14},{3,1},{5,3},... | collective-permute-start | bytes 1585160 | tf_op jit(solution)/shard_map/ppermute | solution.py:289
  91.4 5.7 %collective-permute-done.6.got_r = s16[16,16512]{1,0:T(8,128)(2,1)S(1)} collective-permute-done((s16[16,16512]{1,0:T(8,128)(2,1)S(1)}, s16[16,16512]{1,0:T(8,128)(2,1)S(1)}, u32[]{:S(2)}, u32[]{:S(2)}) %collective-permute-start.6) | collective-permute-done | bytes 528416 | tf_op jit(solution)/shard_map/ppermute | solution.py:289
  97.1 2.6 %turn.1 = s16[16,2,80,128]{3,2,1,0:T(8,128)(2,1)} custom-call(s32[1]{0:T(128)} %bitcast.at, s16[16,16512]{1,0:T(8,128)(2,1)S(1)} %collective-permute-done.6.got_r, s16[16,16512]{1,0:T(8,128)(2,1)S(1)} %collective-permute-done.7.got_l, s16[8,16,16512]{2,1,0:T(8,128)(2,1)} %get-tuple-element.25.parts), custom_call_target="tpu_custom_call" | custom-call | flops 2113536 | bytes 2113536 | tf_op jit(solution)/shard_map/turn/pallas_call | solution.py:338
  99.7 11.0 %all-to-all-start = ((s16[32,80,128]{2,1,0:T(8,128)(2,1)}), s16[32,80,128]{2,1,0:T(8,128)(2,1)S(1)}, u32[]{:S(2)}, u32[]{:S(2)}) async-start(s16[32,80,128]{2,1,0:T(8,128)(2,1)} %bitcast.10), calls=%async_computation | async-start | bytes 1310720 | tf_op jit(solution)/shard_map/all_to_all | solution.py:456
  110.8 2.1 %share.1 = (f32[8,32,512]{2,1,0:T(8,128)S(1)}, s16[16,8320]{1,0:T(8,128)(2,1)S(1)}) custom-call(s32[2]{0:T(128)S(1)} %pad_add_fusion.3.at, s16[16,16512]{1,0:T(8,128)(2,1)S(1)} %collective-permute-done.12.got_r, s16[16,16512]{1,0:T(8,128)(2,1)S(1)} %collective-permute-done.13.got_l, s16[8,16,16512]{2,1,0:T(8,128)(2,1)} %get-tuple-element.32.parts), custom_call_target="tpu_custom_call" | custom-call | flops 2113536 | bytes 2113536 | tf_op jit(solution)/shard_map/share/pallas_call | solution.py:366
  112.9 1.5 %collective-permute-start.14 = (s16[16,8320]{1,0:T(8,128)(2,1)S(1)}, s16[16,8320]{1,0:T(8,128)(2,1)S(1)}, u32[]{:S(2)}, u32[]{:S(2)}) collective-permute-start(s16[16,8320]{1,0:T(8,128)(2,1)S(1)} %get-tuple-element.40), channel_id=1, source_target_pairs={{0,1},{1,0},{2,3},{3,2},{4,5},{5,4},{6,7},{7,6},{8,9},{9,8},{10,11... | collective-permute-start | bytes 798728 | tf_op jit(solution)/shard_map/ppermute | solution.py:444
  114.4 11.3 %collective-permute-done.14.got_0 = s16[16,8320]{1,0:T(8,128)(2,1)S(1)} collective-permute-done((s16[16,8320]{1,0:T(8,128)(2,1)S(1)}, s16[16,8320]{1,0:T(8,128)(2,1)S(1)}, u32[]{:S(2)}, u32[]{:S(2)}) %collective-permute-start.14) | collective-permute-done | bytes 266272 | tf_op jit(solution)/shard_map/ppermute | solution.py:444
  125.7 1.2 last.1
  (19 shorter events, 2.1 us)
Async XLA Ops:
  0.0 2.4 %copy-start = (bf16[100,100,192]{1,2,0:T(8,128)(2,1)S(1)}, bf16[100,100,192]{1,2,0:T(8,128)(2,1)}, u32[]{:S(2)}) copy-start(bf16[100,100,192]{1,2,0:T(8,128)(2,1)} %param.3) | copy-start | bytes 11520004
  2.4 0.7 copy-start.1
  16.8 18.3 %collective-permute-start = (s16[2,16,8320]{2,1,0:T(8,128)(2,1)S(1)}, s16[2,16,8320]{2,1,0:T(8,128)(2,1)S(1)}, u32[]{:S(2)}, u32[]{:S(2)}) collective-permute-start(s16[2,16,8320]{2,1,0:T(8,128)(2,1)S(1)} %get-tuple-element.23), channel_id=1, source_target_pairs={{0,2},{2,4},{4,6},{6,8},{8,10},{10,12},{12,14},{14,0},{1,3},{3,5},... | collective-permute-start | bytes 1597448 | tf_op jit(solution)/shard_map/ppermute | solution.py:282
  19.4 15.8 %collective-permute-start.1 = (s16[2,16,8320]{2,1,0:T(8,128)(2,1)S(1)}, s16[2,16,8320]{2,1,0:T(8,128)(2,1)S(1)}, u32[]{:S(2)}, u32[]{:S(2)}) collective-permute-start(s16[2,16,8320]{2,1,0:T(8,128)(2,1)S(1)} %get-tuple-element.24), channel_id=1, source_target_pairs={{2,0},{4,2},{6,4},{8,6},{10,8},{12,10},{14,12},{0,14},{3,1},{5,3},... | collective-permute-start | bytes 1597448 | tf_op jit(solution)/shard_map/ppermute | solution.py:282
  38.0 13.8 %collective-permute-start.2 = (s16[16,16512]{1,0:T(8,128)(2,1)}, s16[16,16512]{1,0:T(8,128)(2,1)S(1)}, u32[]{:S(2)}, u32[]{:S(2)}) collective-permute-start(s16[16,16512]{1,0:T(8,128)(2,1)} %get-tuple-element.26.after), channel_id=1, source_target_pairs={{0,2},{2,4},{4,6},{6,8},{8,10},{10,12},{12,14},{14,0},{1,3},{3,5},... | collective-permute-start | bytes 1585160 | tf_op jit(solution)/shard_map/ppermute | solution.py:289
  38.1 13.7 %collective-permute-start.3 = (s16[16,16512]{1,0:T(8,128)(2,1)}, s16[16,16512]{1,0:T(8,128)(2,1)S(1)}, u32[]{:S(2)}, u32[]{:S(2)}) collective-permute-start(s16[16,16512]{1,0:T(8,128)(2,1)} %get-tuple-element.27), channel_id=1, source_target_pairs={{2,0},{4,2},{6,4},{8,6},{10,8},{12,10},{14,12},{0,14},{3,1},{5,3},... | collective-permute-start | bytes 1585160 | tf_op jit(solution)/shard_map/ppermute | solution.py:289
  43.7 19.5 %collective-permute-start.8 = (s16[16,16512]{1,0:T(8,128)(2,1)}, s16[16,16512]{1,0:T(8,128)(2,1)S(1)}, u32[]{:S(2)}, u32[]{:S(2)}) collective-permute-start(s16[16,16512]{1,0:T(8,128)(2,1)} %get-tuple-element.33), channel_id=1, source_target_pairs={{0,2},{2,4},{4,6},{6,8},{8,10},{10,12},{12,14},{14,0},{1,3},{3,5},... | collective-permute-start | bytes 1585160 | tf_op jit(solution)/shard_map/ppermute | solution.py:289
  43.8 19.4 %collective-permute-start.9 = (s16[16,16512]{1,0:T(8,128)(2,1)}, s16[16,16512]{1,0:T(8,128)(2,1)S(1)}, u32[]{:S(2)}, u32[]{:S(2)}) collective-permute-start(s16[16,16512]{1,0:T(8,128)(2,1)} %get-tuple-element.34), channel_id=1, source_target_pairs={{2,0},{4,2},{6,4},{8,6},{10,8},{12,10},{14,12},{0,14},{3,1},{5,3},... | collective-permute-start | bytes 1585160 | tf_op jit(solution)/shard_map/ppermute | solution.py:289
  55.1 19.4 %collective-permute-start.4 = (s16[16,16512]{1,0:T(8,128)(2,1)S(1)}, s16[16,16512]{1,0:T(8,128)(2,1)S(1)}, u32[]{:S(2)}, u32[]{:S(2)}) collective-permute-start(s16[16,16512]{1,0:T(8,128)(2,1)S(1)} %get-tuple-element.28.after), channel_id=1, source_target_pairs={{0,2},{2,4},{4,6},{6,8},{8,10},{10,12},{12,14},{14,0},{1,3},{3,5},... | collective-permute-start | bytes 1585160 | tf_op jit(solution)/shard_map/ppermute | solution.py:289
  56.0 18.4 %collective-permute-start.5 = (s16[16,16512]{1,0:T(8,128)(2,1)}, s16[16,16512]{1,0:T(8,128)(2,1)S(1)}, u32[]{:S(2)}, u32[]{:S(2)}) collective-permute-start(s16[16,16512]{1,0:T(8,128)(2,1)} %get-tuple-element.29), channel_id=1, source_target_pairs={{2,0},{4,2},{6,4},{8,6},{10,8},{12,10},{14,12},{0,14},{3,1},{5,3},... | collective-permute-start | bytes 1585160 | tf_op jit(solution)/shard_map/ppermute | solution.py:289
  66.1 19.7 %collective-permute-start.10 = (s16[16,16512]{1,0:T(8,128)(2,1)}, s16[16,16512]{1,0:T(8,128)(2,1)S(1)}, u32[]{:S(2)}, u32[]{:S(2)}) collective-permute-start(s16[16,16512]{1,0:T(8,128)(2,1)} %get-tuple-element.35), channel_id=1, source_target_pairs={{0,2},{2,4},{4,6},{6,8},{8,10},{10,12},{12,14},{14,0},{1,3},{3,5},... | collective-permute-start | bytes 1585160 | tf_op jit(solution)/shard_map/ppermute | solution.py:289
  67.0 18.7 %collective-permute-start.11 = (s16[16,16512]{1,0:T(8,128)(2,1)S(1)}, s16[16,16512]{1,0:T(8,128)(2,1)S(1)}, u32[]{:S(2)}, u32[]{:S(2)}) collective-permute-start(s16[16,16512]{1,0:T(8,128)(2,1)S(1)} %get-tuple-element.36), channel_id=1, source_target_pairs={{2,0},{4,2},{6,4},{8,6},{10,8},{12,10},{14,12},{0,14},{3,1},{5,3},... | collective-permute-start | bytes 1585160 | tf_op jit(solution)/shard_map/ppermute | solution.py:289
  76.9 20.2 %collective-permute-start.6 = (s16[16,16512]{1,0:T(8,128)(2,1)S(1)}, s16[16,16512]{1,0:T(8,128)(2,1)S(1)}, u32[]{:S(2)}, u32[]{:S(2)}) collective-permute-start(s16[16,16512]{1,0:T(8,128)(2,1)S(1)} %get-tuple-element.30.after), channel_id=1, source_target_pairs={{0,2},{2,4},{4,6},{6,8},{8,10},{10,12},{12,14},{14,0},{1,3},{3,5},... | collective-permute-start | bytes 1585160 | tf_op jit(solution)/shard_map/ppermute | solution.py:289
  77.9 19.2 %collective-permute-start.7 = (s16[16,16512]{1,0:T(8,128)(2,1)S(1)}, s16[16,16512]{1,0:T(8,128)(2,1)S(1)}, u32[]{:S(2)}, u32[]{:S(2)}) collective-permute-start(s16[16,16512]{1,0:T(8,128)(2,1)S(1)} %get-tuple-element.31), channel_id=1, source_target_pairs={{2,0},{4,2},{6,4},{8,6},{10,8},{12,10},{14,12},{0,14},{3,1},{5,3},... | collective-permute-start | bytes 1585160 | tf_op jit(solution)/shard_map/ppermute | solution.py:289
  88.6 22.2 %collective-permute-start.12 = (s16[16,16512]{1,0:T(8,128)(2,1)}, s16[16,16512]{1,0:T(8,128)(2,1)S(1)}, u32[]{:S(2)}, u32[]{:S(2)}) collective-permute-start(s16[16,16512]{1,0:T(8,128)(2,1)} %get-tuple-element.37), channel_id=1, source_target_pairs={{0,2},{2,4},{4,6},{6,8},{8,10},{10,12},{12,14},{14,0},{1,3},{3,5},... | collective-permute-start | bytes 1585160 | tf_op jit(solution)/shard_map/ppermute | solution.py:289
  89.6 21.2 %collective-permute-start.13 = (s16[16,16512]{1,0:T(8,128)(2,1)S(1)}, s16[16,16512]{1,0:T(8,128)(2,1)S(1)}, u32[]{:S(2)}, u32[]{:S(2)}) collective-permute-start(s16[16,16512]{1,0:T(8,128)(2,1)S(1)} %get-tuple-element.38), channel_id=1, source_target_pairs={{2,0},{4,2},{6,4},{8,6},{10,8},{12,10},{14,12},{0,14},{3,1},{5,3},... | collective-permute-start | bytes 1585160 | tf_op jit(solution)/shard_map/ppermute | solution.py:289
  99.7 26.0 %all-to-all-start = ((s16[32,80,128]{2,1,0:T(8,128)(2,1)}), s16[32,80,128]{2,1,0:T(8,128)(2,1)S(1)}, u32[]{:S(2)}, u32[]{:S(2)}) async-start(s16[32,80,128]{2,1,0:T(8,128)(2,1)} %bitcast.10), calls=%async_computation | async-start | bytes 1310720 | tf_op jit(solution)/shard_map/all_to_all | solution.py:456
  112.9 12.8 %collective-permute-start.14 = (s16[16,8320]{1,0:T(8,128)(2,1)S(1)}, s16[16,8320]{1,0:T(8,128)(2,1)S(1)}, u32[]{:S(2)}, u32[]{:S(2)}) collective-permute-start(s16[16,8320]{1,0:T(8,128)(2,1)S(1)} %get-tuple-element.40), channel_id=1, source_target_pairs={{0,1},{1,0},{2,3},{3,2},{4,5},{5,4},{6,7},{7,6},{8,9},{9,8},{10,11... | collective-permute-start | bytes 798728 | tf_op jit(solution)/shard_map/ppermute | solution.py:444

commit v3 on v2

v3 whole, which is shorter than its diff:
```python
import functools

import jax
import jax.numpy as jnp
from jax import lax
from jax.experimental import pallas as pl
from jax.experimental.pallas import tpu as pltpu
from jax.sharding import Mesh
from jax.sharding import PartitionSpec as P

OB = 2
PB = OB * OB
A_DEV = 32
AW = 512
F32, I16 = jnp.float32, jnp.int16
ROW, Z, XL = "row", "z", "xl"
LANES = 128
TILES = A_DEV * AW // (16 * LANES)
ROW_W = TILES * LANES
PITCH = A_DEV + 1
TOP = 32700.0
STEPS = 256.0


def params(mib=32):
    return pltpu.CompilerParams(vmem_limit_bytes=mib << 20)


def cost(flops, bytes_accessed):
    return pl.CostEstimate(flops=flops, bytes_accessed=bytes_accessed, transcendentals=0)


def hbm():
    return pl.BlockSpec(memory_space=pltpu.HBM)


def vmem():
    return pl.BlockSpec(memory_space=pltpu.VMEM)


def scale_of(tiles):
    most = functools.reduce(jnp.maximum, [jnp.abs(t) for t in tiles])
    most = jnp.max(most, axis=0, keepdims=True)
    code = jnp.ceil(jnp.log2(jnp.maximum(most, 2.0**-100)) * STEPS)
    return code, TOP * jnp.exp2(code * (-1.0 / STEPS))


def coded(x, factor):
    return jnp.round(x * factor).astype(jnp.int32).astype(I16)


def factors(codes):
    return jnp.exp2(codes.astype(F32) * (1.0 / STEPS)) * (1.0 / TOP)


def column(k, n):
    return k * ROW_W + (LANES if k >= n // 2 else 0)


def get_row(ref, start, factor):
    return [
        ref[:, start + t * LANES : start + (t + 1) * LANES].astype(jnp.int32).astype(F32) * factor
        for t in range(TILES)
    ]


def put_row(ref, start, tiles):
    code, factor = scale_of(tiles)
    for t, tile in enumerate(tiles):
        ref[:, start + t * LANES : start + (t + 1) * LANES] = coded(tile, factor)
    return code


def scale_tile(codes):
    rows = codes + [jnp.zeros((1, LANES), F32)] * (16 - len(codes))
    return jnp.concatenate(rows, axis=0).astype(jnp.int32).astype(I16)


UNROLL = 4


def gather_kernel(z_n, at, blocks, pages, out, picked):
    depth, orbitals = pages.shape[1], pages.shape[2]
    pairs = blocks.shape[1]
    each = pairs // (2 * z_n)
    lane = lax.broadcasted_iota(jnp.int32, (depth, LANES), 1)
    blank = jnp.zeros((depth, LANES - orbitals), F32)
    picked[...] = jnp.zeros_like(picked)

    def turned(page, shift):
        whole = jnp.concatenate([pages[page].astype(F32), blank], axis=1)
        return pltpu.roll(whole, lax.rem(shift + LANES, LANES), 1)

    def some(step, _):
        forward, mirrored = picked[0], picked[1]
        for i in range(UNROLL):
            pair = step * UNROLL + i
            first, second = blocks[0, pair] * OB, blocks[1, pair] * OB
            device, g = pair // each, lax.rem(pair, each)
            z, other = device // 2, lax.rem(device + at[0], 2)
            base_f = (other * z_n + z) * each * PB + g * PB
            for s in range(OB):
                to = base_f + s * OB
                here = (lane >= to) & (lane < to + OB)
                forward = jnp.where(here, turned(first + s, to - second), forward)
                to = pair * PB + s * OB
                here = (lane >= to) & (lane < to + OB)
                mirrored = jnp.where(here, turned(second + s, to - first), mirrored)
        picked[0] = forward
        picked[1] = mirrored
        return 0

    lax.fori_loop(0, pairs // UNROLL, some, 0)
    mirrored = picked[1]
    which = lax.rem(lane, PB)
    mirrored = jnp.where(
        which == 1, pltpu.roll(mirrored, LANES - 1, 1), jnp.where(which == 2, pltpu.roll(mirrored, 1, 1), mirrored)
    )
    out[:LANES] = mirrored.T.astype(out.dtype)
    out[LANES:] = picked[0].T.astype(out.dtype)


def gather(amplitudes, blocks, z_n):
    depth = amplitudes.shape[2]
    rows = blocks.shape[0] * PB
    return pl.pallas_call(
        functools.partial(gather_kernel, z_n),
        out_shape=jax.ShapeDtypeStruct((2 * rows, depth), jnp.bfloat16),
        in_specs=[smem(), smem(), vmem()],
        out_specs=vmem(),
        scratch_shapes=[pltpu.VMEM((2, depth, LANES), F32)],
        compiler_params=params(24),
        name="pick_rows",
    )(lax.axis_index(XL)[None], blocks.T, jnp.swapaxes(amplitudes, 1, 2))


GRID = 8


def fill(left, right, whole):
    step = pl.program_id(0)
    rows = left.shape[0]
    each = A_DEV // GRID
    for i in range(each):
        part = jnp.dot(left[...], right[:, i * AW : (i + 1) * AW], preferred_element_type=F32)
        for c in range(AW // LANES):
            whole[c, pl.ds(step * each + i, rows, stride=PITCH), :] = part[:, c * LANES : (c + 1) * LANES]


def filled(whole, row):
    return [
        whole[c, pl.ds(row * PITCH + h * 16, 16), :] for h in range(2) for c in range(AW // LANES)
    ]


def product_kernel(segments, at, left, right, *refs):
    count = len(segments)
    parts, (out_r, out_l, whole) = refs[:count], refs[count : count + 3]
    coded_rows, sems = refs[count + 3 : 2 * count + 3], refs[-1]
    fill(left, right, whole)

    @pl.when(pl.program_id(0) == GRID - 1)
    def _():
        z_n = parts[0].shape[0]
        first_row = 0
        for i, n in enumerate(segments):
            middle = n // 2 * ROW_W

            def one(z, _, i=i, n=n, first_row=first_row, middle=middle):
                spot = coded_rows[i].at[z]
                codes = [put_row(spot, column(k, n), filled(whole, first_row + z * n + k)) for k in range(n)]
                spot[:, middle : middle + LANES] = scale_tile(codes)
                pltpu.make_async_copy(spot, parts[i].at[z], sems.at[i, z]).start()
                return 0

            lax.fori_loop(0, z_n, one, 0)
            if i == 0:
                opposite = coded_rows[0].at[at[0]]
                out_r[...] = opposite[:, : middle + LANES]
                out_l[...] = opposite[:, middle:]
            first_row += z_n * n
        for i in range(count):
            for z in range(z_n):
                pltpu.make_async_copy(coded_rows[i].at[z], parts[i].at[z], sems.at[i, z]).wait()


def far_side(z_n):
    return lax.rem(lax.axis_index(Z) + z_n // 2, z_n)[None]


def product(left, integrals, z_n, segments):
    rows, depth = left.shape
    width = integrals.shape[1]
    end = jax.ShapeDtypeStruct((16, segments[0] // 2 * ROW_W + LANES), I16)
    shapes = [(z_n, 16, n * ROW_W + LANES) for n in segments]
    return pl.pallas_call(
        functools.partial(product_kernel, segments),
        grid=(GRID,),
        out_shape=[pltpu.HBM(shape, I16) for shape in shapes] + [end, end],
        in_specs=[
            smem(),
            pl.BlockSpec((rows, depth), lambda s: (0, 0)),
            pl.BlockSpec((depth, width // GRID), lambda s: (0, s)),
        ],
        out_specs=[hbm() for _ in shapes] + [pl.BlockSpec(end.shape, lambda s: (0, 0))] * 2,
        scratch_shapes=[pltpu.VMEM(matrices(rows), F32)]
        + [pltpu.VMEM(shape, I16) for shape in shapes]
        + [pltpu.SemaphoreType.DMA((len(segments), z_n))],
        compiler_params=params(48),
        cost_estimate=cost(2 * rows * depth * width, 2 * depth * width + 2 * rows * width),
        name="product",
    )(far_side(z_n), left, in_hbm(integrals))


def in_hbm(x):
    return pltpu.with_memory_space_constraint(x, pltpu.HBM)


def matrices(rows):
    return (AW // LANES, rows * PITCH, LANES)


def smem():
    return pl.BlockSpec(memory_space=pltpu.SMEM)


def anywhere():
    return pl.BlockSpec(memory_space=pl.ANY)


def scales(ref, n):
    middle = n // 2 * ROW_W
    return factors(ref[:, middle : middle + LANES].astype(jnp.int32))


def total_row(refs, scale, k, n):
    rows = [get_row(ref, column(k, n), f[k : k + 1]) for ref, f in zip(refs, scale)]
    return [functools.reduce(jnp.add, tiles) for tiles in zip(*rows)]


def fetch(parts, at, own, sems):
    copies = [pltpu.make_async_copy(part.at[at], own.at[i], sems.at[i]) for i, part in enumerate(parts)]
    for copy in copies:
        copy.start()

    def wait():
        for copy in copies:
            copy.wait()

    return wait


def own_scratch(parts):
    return [pltpu.VMEM((len(parts),) + parts[0].shape[1:], I16), pltpu.SemaphoreType.DMA((len(parts),))]


def open_kernel(n, at, *refs):
    *parts, out_r, out_l, own, sems = refs
    fetch(parts, at[0], own, sems)()
    terms = [own.at[i] for i in range(len(parts))]
    f = [scales(ref, n) for ref in terms]
    half = n // 2
    for out, rows in ((out_r, range(half)), (out_l, range(half, n))):
        start = 0 if out is out_r else LANES
        codes = [jnp.zeros((1, LANES), F32)] * rows[0]
        for i, k in enumerate(rows):
            codes.append(put_row(out, start + i * ROW_W, total_row(terms, f, k, n)))
        spot = half * ROW_W if out is out_r else 0
        out[:, spot : spot + LANES] = scale_tile(codes)


def open_ring(parts, n):
    z_n = parts[0].shape[0]
    end = jax.ShapeDtypeStruct((16, n // 2 * ROW_W + LANES), I16)
    return pl.pallas_call(
        functools.partial(open_kernel, n),
        out_shape=[end, end],
        in_specs=[smem()] + [hbm() for _ in parts],
        out_specs=[vmem(), vmem()],
        scratch_shapes=own_scratch(parts),
        compiler_params=params(16),
        cost_estimate=cost(1000, 3000000),
        name="open_ring",
    )(far_side(z_n), *map(in_hbm, parts))


def step_kernel(n, side, first, at, got, *refs):
    *parts, _, out, own, sems = refs
    half = n // 2
    middle = half * ROW_W
    wait = fetch(parts, at[0], own, sems)
    spot = (middle if side == 0 else 0) if first else middle
    got_f = factors(got[:, spot : spot + LANES].astype(jnp.int32))
    wait()
    terms = [own.at[i] for i in range(len(parts))]
    f = [scales(ref, n) for ref in terms]
    codes = []
    for k in range(n):
        start = column(k, n)
        tiles = total_row(terms, f, k, n)
        if not first or (k < half) == (side == 0):
            came = get_row(got, start - (middle if first and side == 1 else 0), got_f[k : k + 1])
            tiles = [a + b for a, b in zip(tiles, came)]
        codes.append(put_row(out, start, tiles))
    out[:, middle : middle + LANES] = scale_tile(codes)


def ring_step(got, parts, at, n, side, first, after):
    width = parts[0].shape[2]
    return pl.pallas_call(
        functools.partial(step_kernel, n, side, first),
        out_shape=jax.ShapeDtypeStruct((16, width), I16),
        in_specs=[smem(), vmem()] + [hbm() for _ in parts] + [anywhere()],
        out_specs=vmem(),
        scratch_shapes=own_scratch(parts),
        compiler_params=params(16),
        cost_estimate=cost(1000, 3000000),
        name="ring_step",
    )(at, got, *map(in_hbm, parts), after)


def ring(parts, r, l, n):
    z_n = parts[0].shape[0]
    me = lax.axis_index(Z)
    right = [(i, (i + 1) % z_n) for i in range(z_n)]
    left = [((i + 1) % z_n, i) for i in range(z_n)]
    far = z_n // 2
    r, l = lax.ppermute(r, Z, right), lax.ppermute(l, Z, left)
    for d in range(far - 1, 0, -1):
        first = d == far - 1
        at = lax.rem(me + d, z_n)[None]
        r = ring_step(r, parts, at, n, 0, first, at)
        l = ring_step(l, parts, lax.rem(me + z_n - d, z_n)[None], n, 1, first, r)
        r, l = lax.ppermute(r, Z, right), lax.ppermute(l, Z, left)
    return r, l


def matrix(tiles):
    per = len(tiles) // 2
    return jnp.concatenate(
        [jnp.concatenate(tiles[:per], axis=1), jnp.concatenate(tiles[per:], axis=1)], axis=0
    )


def turn_kernel(n, rows_n, at, got_r, got_l, parts, out, own, sems):
    fetch([parts], at[0], own, sems)()
    terms = [got_r, got_l, own.at[0]]
    f = [scales(ref, n) for ref in terms]
    groups = n // (2 * PB)
    for xl in range(2):
        codes = []
        for g in range(groups):
            stack = jnp.concatenate([matrix(total_row(terms, f, (xl * groups + g) * PB + i, n)) for i in range(PB)], axis=0)
            turned = stack.T
            code, factor = scale_of([turned])
            codes.append(code)
            for to in range(rows_n):
                out[to, xl, g * A_DEV : (g + 1) * A_DEV, :] = coded(turned[to * A_DEV : (to + 1) * A_DEV], factor)
        tile = scale_tile(codes)
        for to in range(rows_n):
            out[to, xl, groups * A_DEV : groups * A_DEV + 16, :] = tile


def turn(got_r, got_l, parts, n, rows_n):
    width = parts.shape[2]
    shape = (rows_n, 2, n // (2 * PB) * A_DEV + 16, LANES)
    return pl.pallas_call(
        functools.partial(turn_kernel, n, rows_n),
        out_shape=jax.ShapeDtypeStruct(shape, I16),
        in_specs=[smem(), vmem(), vmem(), hbm()],
        out_specs=vmem(),
        scratch_shapes=own_scratch([parts]),
        compiler_params=params(32),
        cost_estimate=cost(16 * width * 8, 16 * width * 8),
        name="turn",
    )(lax.axis_index(Z)[None], got_r, got_l, in_hbm(parts))


def regroup(tiles):
    count = len(tiles)
    group = LANES // count
    lane = lax.broadcasted_iota(jnp.int32, tiles[0].shape, 1) // group
    out = []
    for k in range(count):
        merged = tiles[k]
        for r in range(count):
            if r != k:
                merged = jnp.where(lane == r, pltpu.roll(tiles[r], (r - k) % count * group, 1), merged)
        out.append(merged)
    return out


def last_kernel(n, rows_n, at, mirrored, r, l, *refs):
    *parts, out, total, own, sems = refs
    wait = fetch(parts, at[0], own, sems)
    groups = n // PB
    spot = groups * A_DEV
    f = [[factors(mirrored[row, s, spot : spot + 16, :].astype(jnp.int32)) for s in range(2)] for row in range(rows_n)]
    for g in range(groups):
        pieces = []
        for row in range(rows_n):
            both = [
                mirrored[row, s, g * A_DEV : (g + 1) * A_DEV, :].astype(jnp.int32).astype(F32) * f[row][s][g : g + 1]
                for s in range(2)
            ]
            pieces.append(both[0] + both[1])
        per = LANES // A_DEV
        for c in range(rows_n // per):
            for i, tile in enumerate(regroup(pieces[c * per : (c + 1) * per])):
                total[c, pl.ds((g * PB + i) * PITCH, A_DEV), :] = tile
    wait()
    terms = [r, l] + [own.at[i] for i in range(len(parts))]
    scale = [scales(ref, n) for ref in terms]
    for k in range(n):
        tiles = total_row(terms, scale, k, n)
        for h in range(2):
            for c in range(AW // LANES):
                total[c, pl.ds(k * PITCH + h * 16, 16), :] += tiles[h * (AW // LANES) + c]
    for a in range(A_DEV):
        for c in range(AW // LANES):
            start = a * AW + c * LANES
            out[:, start : start + LANES] = total[c, pl.ds(a, n, stride=PITCH), :].astype(out.dtype)


def last(mirrored, r, l, parts, n):
    rows_n = mirrored.shape[0]
    return pl.pallas_call(
        functools.partial(last_kernel, n, rows_n),
        out_shape=jax.ShapeDtypeStruct((n, A_DEV * AW), jnp.bfloat16),
        in_specs=[smem(), vmem(), vmem(), vmem()] + [hbm() for _ in parts],
        out_specs=vmem(),
        scratch_shapes=[pltpu.VMEM(matrices(n), F32)] + own_scratch(parts),
        compiler_params=params(16),
        name="last",
    )(lax.axis_index(Z)[None], mirrored, r, l, *map(in_hbm, parts))


def on_device(rows_n, z_n, amplitudes, integrals, blocks):
    picked = gather(amplitudes, blocks, z_n)
    n = picked.shape[0] // (2 * z_n)
    parts, kept, sent, r, l = product(picked, integrals, z_n, (n, n // 2, n // 2))
    got = lax.ppermute(sent, XL, [(0, 1), (1, 0)])
    r, l = ring([parts], r, l, n)
    pieces = turn(r, l, parts, n, rows_n)
    shape = pieces.shape
    pieces = pieces.reshape((rows_n * 2,) + shape[2:])
    pieces = lax.all_to_all(pieces, (ROW, XL), 0, 0, tiled=True).reshape(shape)

    terms = [kept, got]
    r, l = ring(terms, *open_ring(terms, n // 2), n // 2)
    return last(pieces, r, l, terms, n // 2)


def solution(mesh):
    rows_n, cols_n = mesh.devices.shape
    finer = Mesh(mesh.devices.reshape(rows_n, cols_n // 2, 2), (ROW, Z, XL))
    return jax.shard_map(
        functools.partial(on_device, rows_n, cols_n // 2),
        mesh=finer,
        in_specs=(P(None, None, (Z, XL)), P((Z, XL), ROW), P()),
        out_specs=P((Z, XL), ROW),
        check_vma=False,
    )
```

time: 127 us -> 126 us (level); the launches traced: 127 us -> 124 us
  waiting for transfers between devices: 51 us -> 40.6 us
  starting transfers between devices: 35.6 us -> 43.2 us
    ppermute x15 -> x17, waiting for transfers between devices: 51 us -> 40.6 us  [the longest x16 40.6 us: ring(): r, l = (lax.ppermute(r, Z, right), lax.ppermute(l, Z, left))]
    ppermute x15 -> x17, starting transfers between devices: 24.6 us -> 30.9 us  [the longest x16 28.8 us: ring(): r, l = (lax.ppermute(r, Z, right), lax.ppermute(l, Z, left))]
    all_to_all x1, starting transfers between devices: 11 us -> 12.3 us  [on_device(): pieces = lax.all_to_all(pieces, (ROW, XL), 0, 0, tiled=True).reshape(shape)]
    pallas_call x9 -> x15, Pallas kernels: 33.1 us -> 31.9 us  [the longest x12 16.7 us: ring_step(): pl.pallas_call(functools.partial(step_kernel, n, side, first), out_shape=...]
  transfers between devices with their start and end apart: 16 -> 18, of which waited for: 7 -> 7; matrix products, arithmetic and copies ran while one was open for 0% -> 0% of each run, Pallas kernels for 15% -> 17%
where the time goes in v3:
time: 126 us; the launch traced here: 124 us
  starting transfers between devices  43.2 us (34%)
  waiting for transfers between devices  40.6 us (32%)
  Pallas kernels  37 us (29%)
  local copies, waits for them, and re-layouts  3.07 us (2%)
    ppermute x16, waiting for transfers between devices, ring(): r, l = (lax.ppermute(r, Z, right), lax.ppermute(l, Z, left))  40.6 us
    ppermute x16, starting transfers between devices, ring(): r, l = (lax.ppermute(r, Z, right), lax.ppermute(l, Z, left))  28.8 us
    pallas_call x12, Pallas kernels, ring_step(): pl.pallas_call(functools.partial(step_kernel, n, side, first), out_shape=...  16.7 us
    all_to_all x1, starting transfers between devices, on_device(): pieces = lax.all_to_all(pieces, (ROW, XL), 0, 0, tiled=True).reshape(shape)  12.3 us
    pallas_call x1, Pallas kernels, product(): pl.pallas_call(functools.partial(product_kernel, segments), grid=(GRID,),...  10.9 us
    pallas_call x1, Pallas kernels, gather(): pl.pallas_call(functools.partial(gather_kernel, z_n), out_shape=jax.Shape...  3.11 us
    unnamed x4, local copies, waits for them, and re-layouts  3.07 us
    pallas_call x1, Pallas kernels, turn(): pl.pallas_call(functools.partial(turn_kernel, n, rows_n), out_shape=jax.S...  2.57 us
  transfers between devices with their start and end apart: 18, of which 7 were waited for; matrix products, arithmetic and copies ran while one was open for 0% of the time, Pallas kernels for 17%

profile of v3, /device:TPU:1, one launch (start us, length us, event | category | flops | bytes accessed | tf_op | source)
XLA Modules:
  0.0 124.2 jit_solution(13549368386943364736)
XLA Ops:
  0.0 2.4 %copy-done = bf16[100,100,192]{1,2,0:T(8,128)(2,1)S(1)} copy-done((bf16[100,100,192]{1,2,0:T(8,128)(2,1)S(1)}, bf16[100,100,192]{1,2,0:T(8,128)(2,1)}, u32[]{:S(2)}) %copy-start) | copy-done | bytes 3840024
  3.1 3.1 %pick_rows.1.left = bf16[256,192]{1,0:T(8,128)(2,1)S(1)} custom-call(s32[1]{0:T(128)} %bitcast.5.at, s32[2,32]{1,0:T(2,128)S(1)} %bitcast.15, bf16[100,192,100]{2,1,0:T(8,128)(2,1)S(1)} %bitcast.13), custom_call_target="tpu_custom_call" | custom-call | tf_op jit(solution)/shard_map/pick_rows/pallas_call | solution.py:126
  6.2 10.9 %product.1 = (s16[8,16,16512]{2,1,0:T(8,128)(2,1)}, s16[8,16,8320]{2,1,0:T(8,128)(2,1)}, s16[8,16,8320]{2,1,0:T(8,128)(2,1)}, s16[16,8320]{1,0:T(8,128)(2,1)S(1)}, s16[16,8320]{1,0:T(8,128)(2,1)S(1)}) custom-call(s32[1]{0:T(128)} %bitcast.4.at, bf16[256,192]{1,0:T(8,128)(2,1)S(1)} %pick_rows.1.left, bf16[192,16384]{1,0:T(8,128)(2,1)} %right.1), custom_call_target="tpu_custom_call" | custom-call | flops 1610612736 | bytes 14680064 | tf_op jit(solution)/shard_map/product/pallas_call | solution.py:196
  17.1 2.1 %collective-permute-start.8 = (s16[8,16,8320]{2,1,0:T(8,128)(2,1)}, s16[8,16,8320]{2,1,0:T(8,128)(2,1)}, u32[]{:S(2)}, u32[]{:S(2)}) collective-permute-start(s16[8,16,8320]{2,1,0:T(8,128)(2,1)} %get-tuple-element.16), channel_id=1, source_target_pairs={{0,1},{1,0},{2,3},{3,2},{4,5},{5,4},{6,7},{7,6},{8,9},{9,8},{10,11... | collective-permute-start | bytes 6389768 | tf_op jit(solution)/shard_map/ppermute | solution.py:442
  19.2 1.6 %collective-permute-start = (s16[16,8320]{1,0:T(8,128)(2,1)S(1)}, s16[16,8320]{1,0:T(8,128)(2,1)S(1)}, u32[]{:S(2)}, u32[]{:S(2)}) collective-permute-start(s16[16,8320]{1,0:T(8,128)(2,1)S(1)} %get-tuple-element.12), channel_id=1, source_target_pairs={{0,2},{2,4},{4,6},{6,8},{8,10},{10,12},{12,14},{14,0},{1,3},{3,5},... | collective-permute-start | bytes 798728 | tf_op jit(solution)/shard_map/ppermute | solution.py:328
  20.8 3.9 %collective-permute-start.4 = (s16[16,8320]{1,0:T(8,128)(2,1)S(1)}, s16[16,8320]{1,0:T(8,128)(2,1)S(1)}, u32[]{:S(2)}, u32[]{:S(2)}) collective-permute-start(s16[16,8320]{1,0:T(8,128)(2,1)S(1)} %get-tuple-element.14), channel_id=1, source_target_pairs={{2,0},{4,2},{6,4},{8,6},{10,8},{12,10},{14,12},{0,14},{3,1},{5,3},... | collective-permute-start | bytes 798728 | tf_op jit(solution)/shard_map/ppermute | solution.py:328
  24.8 5.8 %collective-permute-done.got = s16[16,8320]{1,0:T(8,128)(2,1)S(1)} collective-permute-done((s16[16,8320]{1,0:T(8,128)(2,1)S(1)}, s16[16,8320]{1,0:T(8,128)(2,1)S(1)}, u32[]{:S(2)}, u32[]{:S(2)}) %collective-permute-start) | collective-permute-done | bytes 266272 | tf_op jit(solution)/shard_map/ppermute | solution.py:328
  30.6 1.4 %ring_step.12.refs_1_ = s16[16,16512]{1,0:T(8,128)(2,1)S(1)} custom-call(s32[1]{0:T(128)} %bitcast.3.at.refs_1_.refs_2_, s16[16,8320]{1,0:T(8,128)(2,1)S(1)} %collective-permute-done.got, s16[8,16,16512]{2,1,0:T(8,128)(2,1)} %get-tuple-element.13.refs_0_.parts, s32[1]{0:T(128)} %bitcast.3.at.refs_1_.refs_2_), custom_call_target="tpu_custom_call" | custom-call | flops 1000 | bytes 3000000 | tf_op jit(solution)/shard_map/ring_step/pallas_call | solution.py:310
  32.1 1.4 %ring_step.15 = s16[16,16512]{1,0:T(8,128)(2,1)S(1)} custom-call(s32[1]{0:T(128)} %bitcast.10.at, s16[16,8320]{1,0:T(8,128)(2,1)S(1)} %collective-permute-done.4.got, s16[8,16,16512]{2,1,0:T(8,128)(2,1)} %get-tuple-element.13.refs_0_.parts, s16[16,16512]{1,0:T(8,128)(2,1)S(1)} %ring_step.12.refs_1_), custom_call_target="tpu_custom_call" | custom-call | flops 1000 | bytes 3000000 | tf_op jit(solution)/shard_map/ring_step/pallas_call | solution.py:310
  33.5 2.7 %collective-permute-start.5 = (s16[16,16512]{1,0:T(8,128)(2,1)S(1)}, s16[16,16512]{1,0:T(8,128)(2,1)S(1)}, u32[]{:S(2)}, u32[]{:S(2)}) collective-permute-start(s16[16,16512]{1,0:T(8,128)(2,1)S(1)} %ring_step.15), channel_id=1, source_target_pairs={{2,0},{4,2},{6,4},{8,6},{10,8},{12,10},{14,12},{0,14},{3,1},{5,3},... | collective-permute-start | bytes 1585160 | tf_op jit(solution)/shard_map/ppermute | solution.py:334
  36.2 9.0 %collective-permute-done.1.got = s16[16,16512]{1,0:T(8,128)(2,1)S(1)} collective-permute-done((s16[16,16512]{1,0:T(8,128)(2,1)S(1)}, s16[16,16512]{1,0:T(8,128)(2,1)S(1)}, u32[]{:S(2)}, u32[]{:S(2)}) %collective-permute-start.1) | collective-permute-done | bytes 528416 | tf_op jit(solution)/shard_map/ppermute | solution.py:334
  45.2 1.5 %ring_step.13.refs_1_ = s16[16,16512]{1,0:T(8,128)(2,1)S(1)} custom-call(s32[1]{0:T(128)} %bitcast.2.at.refs_1_.refs_2_, s16[16,16512]{1,0:T(8,128)(2,1)S(1)} %collective-permute-done.1.got, s16[8,16,16512]{2,1,0:T(8,128)(2,1)} %get-tuple-element.13.refs_0_.parts, s32[1]{0:T(128)} %bitcast.2.at.refs_1_.refs_2_), custom_call_target="tpu_custom_call" | custom-call | flops 1000 | bytes 3000000 | tf_op jit(solution)/shard_map/ring_step/pallas_call | solution.py:310
  46.8 1.5 %ring_step.16 = s16[16,16512]{1,0:T(8,128)(2,1)S(1)} custom-call(s32[1]{0:T(128)} %bitcast.9.at, s16[16,16512]{1,0:T(8,128)(2,1)S(1)} %collective-permute-done.5.got, s16[8,16,16512]{2,1,0:T(8,128)(2,1)} %get-tuple-element.13.refs_0_.parts, s16[16,16512]{1,0:T(8,128)(2,1)S(1)} %ring_step.13.refs_1_), custom_call_target="tpu_custom_call" | custom-call | flops 1000 | bytes 3000000 | tf_op jit(solution)/shard_map/ring_step/pallas_call | solution.py:310
  48.3 2.7 %collective-permute-start.6 = (s16[16,16512]{1,0:T(8,128)(2,1)S(1)}, s16[16,16512]{1,0:T(8,128)(2,1)S(1)}, u32[]{:S(2)}, u32[]{:S(2)}) collective-permute-start(s16[16,16512]{1,0:T(8,128)(2,1)S(1)} %ring_step.16), channel_id=1, source_target_pairs={{2,0},{4,2},{6,4},{8,6},{10,8},{12,10},{14,12},{0,14},{3,1},{5,3},... | collective-permute-start | bytes 1585160 | tf_op jit(solution)/shard_map/ppermute | solution.py:334
  51.0 8.0 %collective-permute-done.2.got = s16[16,16512]{1,0:T(8,128)(2,1)S(1)} collective-permute-done((s16[16,16512]{1,0:T(8,128)(2,1)S(1)}, s16[16,16512]{1,0:T(8,128)(2,1)S(1)}, u32[]{:S(2)}, u32[]{:S(2)}) %collective-permute-start.2) | collective-permute-done | bytes 528416 | tf_op jit(solution)/shard_map/ppermute | solution.py:334
  59.0 1.5 %ring_step.14.refs_1_ = s16[16,16512]{1,0:T(8,128)(2,1)S(1)} custom-call(s32[1]{0:T(128)} %bitcast.1.at.refs_1_.refs_2_, s16[16,16512]{1,0:T(8,128)(2,1)S(1)} %collective-permute-done.2.got, s16[8,16,16512]{2,1,0:T(8,128)(2,1)} %get-tuple-element.13.refs_0_.parts, s32[1]{0:T(128)} %bitcast.1.at.refs_1_.refs_2_), custom_call_target="tpu_custom_call" | custom-call | flops 1000 | bytes 3000000 | tf_op jit(solution)/shard_map/ring_step/pallas_call | solution.py:310
  60.5 1.5 %ring_step.17 = s16[16,16512]{1,0:T(8,128)(2,1)S(1)} custom-call(s32[1]{0:T(128)} %bitcast.8.at, s16[16,16512]{1,0:T(8,128)(2,1)S(1)} %collective-permute-done.6.got, s16[8,16,16512]{2,1,0:T(8,128)(2,1)} %get-tuple-element.13.refs_0_.parts, s16[16,16512]{1,0:T(8,128)(2,1)S(1)} %ring_step.14.refs_1_), custom_call_target="tpu_custom_call" | custom-call | flops 1000 | bytes 3000000 | tf_op jit(solution)/shard_map/ring_step/pallas_call | solution.py:310
  62.0 2.5 %collective-permute-start.7 = (s16[16,16512]{1,0:T(8,128)(2,1)S(1)}, s16[16,16512]{1,0:T(8,128)(2,1)S(1)}, u32[]{:S(2)}, u32[]{:S(2)}) collective-permute-start(s16[16,16512]{1,0:T(8,128)(2,1)S(1)} %ring_step.17), channel_id=1, source_target_pairs={{2,0},{4,2},{6,4},{8,6},{10,8},{12,10},{14,12},{0,14},{3,1},{5,3},... | collective-permute-start | bytes 1585160 | tf_op jit(solution)/shard_map/ppermute | solution.py:334
  65.8 2.7 %collective-permute-start.9 = (s16[16,4224]{1,0:T(8,128)(2,1)S(1)}, s16[16,4224]{1,0:T(8,128)(2,1)S(1)}, u32[]{:S(2)}, u32[]{:S(2)}) collective-permute-start(s16[16,4224]{1,0:T(8,128)(2,1)S(1)} %get-tuple-element.17), channel_id=1, source_target_pairs={{0,2},{2,4},{4,6},{6,8},{8,10},{10,12},{12,14},{14,0},{1,3},{3,5},... | collective-permute-start | bytes 405512 | tf_op jit(solution)/shard_map/ppermute | solution.py:328
  68.5 4.2 %collective-permute-start.13 = (s16[16,4224]{1,0:T(8,128)(2,1)S(1)}, s16[16,4224]{1,0:T(8,128)(2,1)S(1)}, u32[]{:S(2)}, u32[]{:S(2)}) collective-permute-start(s16[16,4224]{1,0:T(8,128)(2,1)S(1)} %get-tuple-element.18), channel_id=1, source_target_pairs={{2,0},{4,2},{6,4},{8,6},{10,8},{12,10},{14,12},{0,14},{3,1},{5,3},... | collective-permute-start | bytes 405512 | tf_op jit(solution)/shard_map/ppermute | solution.py:328
  72.7 5.5 %collective-permute-done.9.got = s16[16,4224]{1,0:T(8,128)(2,1)S(1)} collective-permute-done((s16[16,4224]{1,0:T(8,128)(2,1)S(1)}, s16[16,4224]{1,0:T(8,128)(2,1)S(1)}, u32[]{:S(2)}, u32[]{:S(2)}) %collective-permute-start.9) | collective-permute-done | bytes 135200 | tf_op jit(solution)/shard_map/ppermute | solution.py:328
  80.9 2.7 %collective-permute-start.14 = (s16[16,8320]{1,0:T(8,128)(2,1)S(1)}, s16[16,8320]{1,0:T(8,128)(2,1)S(1)}, u32[]{:S(2)}, u32[]{:S(2)}) collective-permute-start(s16[16,8320]{1,0:T(8,128)(2,1)S(1)} %ring_step.21), channel_id=1, source_target_pairs={{2,0},{4,2},{6,4},{8,6},{10,8},{12,10},{14,12},{0,14},{3,1},{5,3},... | collective-permute-start | bytes 798728 | tf_op jit(solution)/shard_map/ppermute | solution.py:334
  83.6 2.6 %turn.1 = s16[16,2,80,128]{3,2,1,0:T(8,128)(2,1)} custom-call(s32[1]{0:T(128)} %bitcast.at, s16[16,16512]{1,0:T(8,128)(2,1)S(1)} %collective-permute-done.3.got_r, s16[16,16512]{1,0:T(8,128)(2,1)S(1)} %collective-permute-done.7.got_l, s16[8,16,16512]{2,1,0:T(8,128)(2,1)} %get-tuple-element.13.refs_0_.parts), custom_call_target="tpu_custom_call" | custom-call | flops 2113536 | bytes 2113536 | tf_op jit(solution)/shard_map/turn/pallas_call | solution.py:367
  86.2 12.3 %all-to-all-start = ((s16[32,80,128]{2,1,0:T(8,128)(2,1)}), s16[32,80,128]{2,1,0:T(8,128)(2,1)S(1)}, u32[]{:S(2)}, u32[]{:S(2)}) async-start(s16[32,80,128]{2,1,0:T(8,128)(2,1)} %bitcast.11), calls=%async_computation | async-start | bytes 1310720 | tf_op jit(solution)/shard_map/all_to_all | solution.py:447
  98.5 1.3 %ring_step.19.refs_2_ = s16[16,8320]{1,0:T(8,128)(2,1)S(1)} custom-call(s32[1]{0:T(128)} %bitcast.2.at.refs_1_.refs_2_, s16[16,8320]{1,0:T(8,128)(2,1)S(1)} %collective-permute-done.10.got, s16[8,16,8320]{2,1,0:T(8,128)(2,1)} %get-tuple-element.15.refs_0_, s16[8,16,8320]{2,1,0:T(8,128)(2,1)} %collective-permute-done.8.refs_1_, s32[1]{0:T(128)} %bitcast.2.at.refs_1_.refs_2_), custom_call_target="tpu_custom_call" | custom-call | flops 1000 | bytes 3000000 | tf_op jit(solution)/shard_map/ring_step/pallas_call | solution.py:310
  100.0 1.3 %ring_step.22 = s16[16,8320]{1,0:T(8,128)(2,1)S(1)} custom-call(s32[1]{0:T(128)} %bitcast.9.at, s16[16,8320]{1,0:T(8,128)(2,1)S(1)} %collective-permute-done.14.got, s16[8,16,8320]{2,1,0:T(8,128)(2,1)} %get-tuple-element.15.refs_0_, s16[8,16,8320]{2,1,0:T(8,128)(2,1)} %collective-permute-done.8.refs_1_, s16[16,8320]{1,0:T(8,128)(2,1)S(1)} %ring_step.19.refs_2_), custom_call_target="tpu_custom_call" | custom-call | flops 1000 | bytes 3000000 | tf_op jit(solution)/shard_map/ring_step/pallas_call | solution.py:310
  101.3 2.7 %collective-permute-start.15 = (s16[16,8320]{1,0:T(8,128)(2,1)S(1)}, s16[16,8320]{1,0:T(8,128)(2,1)S(1)}, u32[]{:S(2)}, u32[]{:S(2)}) collective-permute-start(s16[16,8320]{1,0:T(8,128)(2,1)S(1)} %ring_step.22), channel_id=1, source_target_pairs={{2,0},{4,2},{6,4},{8,6},{10,8},{12,10},{14,12},{0,14},{3,1},{5,3},... | collective-permute-start | bytes 798728 | tf_op jit(solution)/shard_map/ppermute | solution.py:334
  104.0 4.9 %collective-permute-done.11.got = s16[16,8320]{1,0:T(8,128)(2,1)S(1)} collective-permute-done((s16[16,8320]{1,0:T(8,128)(2,1)S(1)}, s16[16,8320]{1,0:T(8,128)(2,1)S(1)}, u32[]{:S(2)}, u32[]{:S(2)}) %collective-permute-start.11) | collective-permute-done | bytes 266272 | tf_op jit(solution)/shard_map/ppermute | solution.py:334
  111.6 2.5 %collective-permute-start.16 = (s16[16,8320]{1,0:T(8,128)(2,1)S(1)}, s16[16,8320]{1,0:T(8,128)(2,1)S(1)}, u32[]{:S(2)}, u32[]{:S(2)}) collective-permute-start(s16[16,8320]{1,0:T(8,128)(2,1)S(1)} %ring_step.23), channel_id=1, source_target_pairs={{2,0},{4,2},{6,4},{8,6},{10,8},{12,10},{14,12},{0,14},{3,1},{5,3},... | collective-permute-start | bytes 798728 | tf_op jit(solution)/shard_map/ppermute | solution.py:334
  114.1 4.4 %collective-permute-done.16.l = s16[16,8320]{1,0:T(8,128)(2,1)S(1)} collective-permute-done((s16[16,8320]{1,0:T(8,128)(2,1)S(1)}, s16[16,8320]{1,0:T(8,128)(2,1)S(1)}, u32[]{:S(2)}, u32[]{:S(2)}) %collective-permute-start.16) | collective-permute-done | bytes 266272 | tf_op jit(solution)/shard_map/ppermute | solution.py:334
  118.5 3.0 %collective-permute-done.12.r = s16[16,8320]{1,0:T(8,128)(2,1)S(1)} collective-permute-done((s16[16,8320]{1,0:T(8,128)(2,1)S(1)}, s16[16,8320]{1,0:T(8,128)(2,1)S(1)}, u32[]{:S(2)}, u32[]{:S(2)}) %collective-permute-start.12) | collective-permute-done | bytes 266272 | tf_op jit(solution)/shard_map/ppermute | solution.py:334
  121.6 2.5 %last.1 = bf16[8,16384]{1,0:T(8,128)(2,1)} custom-call(s32[1]{0:T(128)} %bitcast.at, s16[16,2,80,128]{3,2,1,0:T(8,128)(2,1)S(1)} %bitcast.14, s16[16,8320]{1,0:T(8,128)(2,1)S(1)} %collective-permute-done.12.r, s16[16,8320]{1,0:T(8,128)(2,1)S(1)} %collective-permute-done.16.l, s16[8,16,8320]{2,1,0:T(8,128)(2,1)} %get-tuple-element.15.refs_0_, ...), custom_call_target="tpu_custom_call" | custom-call | tf_op jit(solution)/shard_map/last/pallas_call | solution.py:427
  (25 shorter events, 7.6 us)
Async XLA Ops:
  0.0 2.4 %copy-start = (bf16[100,100,192]{1,2,0:T(8,128)(2,1)S(1)}, bf16[100,100,192]{1,2,0:T(8,128)(2,1)}, u32[]{:S(2)}) copy-start(bf16[100,100,192]{1,2,0:T(8,128)(2,1)} %param.3) | copy-start | bytes 11520004
  2.4 0.7 copy-start.1
  17.1 47.4 %collective-permute-start.8 = (s16[8,16,8320]{2,1,0:T(8,128)(2,1)}, s16[8,16,8320]{2,1,0:T(8,128)(2,1)}, u32[]{:S(2)}, u32[]{:S(2)}) collective-permute-start(s16[8,16,8320]{2,1,0:T(8,128)(2,1)} %get-tuple-element.16), channel_id=1, source_target_pairs={{0,1},{1,0},{2,3},{3,2},{4,5},{5,4},{6,7},{7,6},{8,9},{9,8},{10,11... | collective-permute-start | bytes 6389768 | tf_op jit(solution)/shard_map/ppermute | solution.py:442
  19.2 11.4 %collective-permute-start = (s16[16,8320]{1,0:T(8,128)(2,1)S(1)}, s16[16,8320]{1,0:T(8,128)(2,1)S(1)}, u32[]{:S(2)}, u32[]{:S(2)}) collective-permute-start(s16[16,8320]{1,0:T(8,128)(2,1)S(1)} %get-tuple-element.12), channel_id=1, source_target_pairs={{0,2},{2,4},{4,6},{6,8},{8,10},{10,12},{12,14},{14,0},{1,3},{3,5},... | collective-permute-start | bytes 798728 | tf_op jit(solution)/shard_map/ppermute | solution.py:328
  20.8 11.2 %collective-permute-start.4 = (s16[16,8320]{1,0:T(8,128)(2,1)S(1)}, s16[16,8320]{1,0:T(8,128)(2,1)S(1)}, u32[]{:S(2)}, u32[]{:S(2)}) collective-permute-start(s16[16,8320]{1,0:T(8,128)(2,1)S(1)} %get-tuple-element.14), channel_id=1, source_target_pairs={{2,0},{4,2},{6,4},{8,6},{10,8},{12,10},{14,12},{0,14},{3,1},{5,3},... | collective-permute-start | bytes 798728 | tf_op jit(solution)/shard_map/ppermute | solution.py:328
  32.0 13.2 %collective-permute-start.1 = (s16[16,16512]{1,0:T(8,128)(2,1)S(1)}, s16[16,16512]{1,0:T(8,128)(2,1)S(1)}, u32[]{:S(2)}, u32[]{:S(2)}) collective-permute-start(s16[16,16512]{1,0:T(8,128)(2,1)S(1)} %ring_step.12.refs_1_), channel_id=1, source_target_pairs={{0,2},{2,4},{4,6},{6,8},{8,10},{10,12},{12,14},{14,0},{1,3},{3,5},... | collective-permute-start | bytes 1585160 | tf_op jit(solution)/shard_map/ppermute | solution.py:334
  33.5 13.3 %collective-permute-start.5 = (s16[16,16512]{1,0:T(8,128)(2,1)S(1)}, s16[16,16512]{1,0:T(8,128)(2,1)S(1)}, u32[]{:S(2)}, u32[]{:S(2)}) collective-permute-start(s16[16,16512]{1,0:T(8,128)(2,1)S(1)} %ring_step.15), channel_id=1, source_target_pairs={{2,0},{4,2},{6,4},{8,6},{10,8},{12,10},{14,12},{0,14},{3,1},{5,3},... | collective-permute-start | bytes 1585160 | tf_op jit(solution)/shard_map/ppermute | solution.py:334
  46.7 12.3 %collective-permute-start.2 = (s16[16,16512]{1,0:T(8,128)(2,1)S(1)}, s16[16,16512]{1,0:T(8,128)(2,1)S(1)}, u32[]{:S(2)}, u32[]{:S(2)}) collective-permute-start(s16[16,16512]{1,0:T(8,128)(2,1)S(1)} %ring_step.13.refs_1_), channel_id=1, source_target_pairs={{0,2},{2,4},{4,6},{6,8},{8,10},{10,12},{12,14},{14,0},{1,3},{3,5},... | collective-permute-start | bytes 1585160 | tf_op jit(solution)/shard_map/ppermute | solution.py:334
  48.3 12.2 %collective-permute-start.6 = (s16[16,16512]{1,0:T(8,128)(2,1)S(1)}, s16[16,16512]{1,0:T(8,128)(2,1)S(1)}, u32[]{:S(2)}, u32[]{:S(2)}) collective-permute-start(s16[16,16512]{1,0:T(8,128)(2,1)S(1)} %ring_step.16), channel_id=1, source_target_pairs={{2,0},{4,2},{6,4},{8,6},{10,8},{12,10},{14,12},{0,14},{3,1},{5,3},... | collective-permute-start | bytes 1585160 | tf_op jit(solution)/shard_map/ppermute | solution.py:334
  62.0 21.7 %collective-permute-start.7 = (s16[16,16512]{1,0:T(8,128)(2,1)S(1)}, s16[16,16512]{1,0:T(8,128)(2,1)S(1)}, u32[]{:S(2)}, u32[]{:S(2)}) collective-permute-start(s16[16,16512]{1,0:T(8,128)(2,1)S(1)} %ring_step.17), channel_id=1, source_target_pairs={{2,0},{4,2},{6,4},{8,6},{10,8},{12,10},{14,12},{0,14},{3,1},{5,3},... | collective-permute-start | bytes 1585160 | tf_op jit(solution)/shard_map/ppermute | solution.py:334
  64.5 19.1 %collective-permute-start.3 = (s16[16,16512]{1,0:T(8,128)(2,1)S(1)}, s16[16,16512]{1,0:T(8,128)(2,1)S(1)}, u32[]{:S(2)}, u32[]{:S(2)}) collective-permute-start(s16[16,16512]{1,0:T(8,128)(2,1)S(1)} %ring_step.14.refs_1_), channel_id=1, source_target_pairs={{0,2},{2,4},{4,6},{6,8},{8,10},{10,12},{12,14},{14,0},{1,3},{3,5},... | collective-permute-start | bytes 1585160 | tf_op jit(solution)/shard_map/ppermute | solution.py:334
  65.8 12.4 %collective-permute-start.9 = (s16[16,4224]{1,0:T(8,128)(2,1)S(1)}, s16[16,4224]{1,0:T(8,128)(2,1)S(1)}, u32[]{:S(2)}, u32[]{:S(2)}) collective-permute-start(s16[16,4224]{1,0:T(8,128)(2,1)S(1)} %get-tuple-element.17), channel_id=1, source_target_pairs={{0,2},{2,4},{4,6},{6,8},{8,10},{10,12},{12,14},{14,0},{1,3},{3,5},... | collective-permute-start | bytes 405512 | tf_op jit(solution)/shard_map/ppermute | solution.py:328
  68.5 11.1 %collective-permute-start.13 = (s16[16,4224]{1,0:T(8,128)(2,1)S(1)}, s16[16,4224]{1,0:T(8,128)(2,1)S(1)}, u32[]{:S(2)}, u32[]{:S(2)}) collective-permute-start(s16[16,4224]{1,0:T(8,128)(2,1)S(1)} %get-tuple-element.18), channel_id=1, source_target_pairs={{2,0},{4,2},{6,4},{8,6},{10,8},{12,10},{14,12},{0,14},{3,1},{5,3},... | collective-permute-start | bytes 405512 | tf_op jit(solution)/shard_map/ppermute | solution.py:328
  79.5 19.0 %collective-permute-start.10 = (s16[16,8320]{1,0:T(8,128)(2,1)S(1)}, s16[16,8320]{1,0:T(8,128)(2,1)S(1)}, u32[]{:S(2)}, u32[]{:S(2)}) collective-permute-start(s16[16,8320]{1,0:T(8,128)(2,1)S(1)} %ring_step.18.refs_2_), channel_id=1, source_target_pairs={{0,2},{2,4},{4,6},{6,8},{8,10},{10,12},{12,14},{14,0},{1,3},{3,5},... | collective-permute-start | bytes 798728 | tf_op jit(solution)/shard_map/ppermute | solution.py:334
  80.9 19.1 %collective-permute-start.14 = (s16[16,8320]{1,0:T(8,128)(2,1)S(1)}, s16[16,8320]{1,0:T(8,128)(2,1)S(1)}, u32[]{:S(2)}, u32[]{:S(2)}) collective-permute-start(s16[16,8320]{1,0:T(8,128)(2,1)S(1)} %ring_step.21), channel_id=1, source_target_pairs={{2,0},{4,2},{6,4},{8,6},{10,8},{12,10},{14,12},{0,14},{3,1},{5,3},... | collective-permute-start | bytes 798728 | tf_op jit(solution)/shard_map/ppermute | solution.py:334
  86.2 27.9 %all-to-all-start = ((s16[32,80,128]{2,1,0:T(8,128)(2,1)}), s16[32,80,128]{2,1,0:T(8,128)(2,1)S(1)}, u32[]{:S(2)}, u32[]{:S(2)}) async-start(s16[32,80,128]{2,1,0:T(8,128)(2,1)} %bitcast.11), calls=%async_computation | async-start | bytes 1310720 | tf_op jit(solution)/shard_map/all_to_all | solution.py:447
  99.9 9.1 %collective-permute-start.11 = (s16[16,8320]{1,0:T(8,128)(2,1)S(1)}, s16[16,8320]{1,0:T(8,128)(2,1)S(1)}, u32[]{:S(2)}, u32[]{:S(2)}) collective-permute-start(s16[16,8320]{1,0:T(8,128)(2,1)S(1)} %ring_step.19.refs_2_), channel_id=1, source_target_pairs={{0,2},{2,4},{4,6},{6,8},{8,10},{10,12},{12,14},{14,0},{1,3},{3,5},... | collective-permute-start | bytes 798728 | tf_op jit(solution)/shard_map/ppermute | solution.py:334
  101.3 8.9 %collective-permute-start.15 = (s16[16,8320]{1,0:T(8,128)(2,1)S(1)}, s16[16,8320]{1,0:T(8,128)(2,1)S(1)}, u32[]{:S(2)}, u32[]{:S(2)}) collective-permute-start(s16[16,8320]{1,0:T(8,128)(2,1)S(1)} %ring_step.22), channel_id=1, source_target_pairs={{2,0},{4,2},{6,4},{8,6},{10,8},{12,10},{14,12},{0,14},{3,1},{5,3},... | collective-permute-start | bytes 798728 | tf_op jit(solution)/shard_map/ppermute | solution.py:334
  111.6 6.9 %collective-permute-start.16 = (s16[16,8320]{1,0:T(8,128)(2,1)S(1)}, s16[16,8320]{1,0:T(8,128)(2,1)S(1)}, u32[]{:S(2)}, u32[]{:S(2)}) collective-permute-start(s16[16,8320]{1,0:T(8,128)(2,1)S(1)} %ring_step.23), channel_id=1, source_target_pairs={{2,0},{4,2},{6,4},{8,6},{10,8},{12,10},{14,12},{0,14},{3,1},{5,3},... | collective-permute-start | bytes 798728 | tf_op jit(solution)/shard_map/ppermute | solution.py:334
  114.1 7.5 %collective-permute-start.12 = (s16[16,8320]{1,0:T(8,128)(2,1)S(1)}, s16[16,8320]{1,0:T(8,128)(2,1)S(1)}, u32[]{:S(2)}, u32[]{:S(2)}) collective-permute-start(s16[16,8320]{1,0:T(8,128)(2,1)S(1)} %ring_step.20.refs_2_), channel_id=1, source_target_pairs={{0,2},{2,4},{4,6},{6,8},{8,10},{10,12},{12,14},{14,0},{1,3},{3,5},... | collective-permute-start | bytes 798728 | tf_op jit(solution)/shard_map/ppermute | solution.py:334

commit v4 on v3

--- a/solution.py
+++ b/solution.py
@@ -134,7 +134,7 @@
     )(lax.axis_index(XL)[None], blocks.T, jnp.swapaxes(amplitudes, 1, 2))
 
 
-GRID = 8
+GRID = 4
 
 
 def fill(left, right, whole):

time: 126 us -> 124 us (0.984)
  Pallas kernels: 37 us -> 35.2 us
    pallas_call x1, Pallas kernels: 10.9 us -> 9.08 us  [product(): pl.pallas_call(functools.partial(product_kernel, segments), grid=(GRID,),...]
where the time goes in v4:
time: 124 us; the launch traced here: 122 us
  starting transfers between devices  43.1 us (35%)
  waiting for transfers between devices  40.7 us (33%)
  Pallas kernels  35.2 us (28%)
  local copies, waits for them, and re-layouts  3.07 us (2%)
    ppermute x16, waiting for transfers between devices, ring(): r, l = (lax.ppermute(r, Z, right), lax.ppermute(l, Z, left))  40.6 us
    ppermute x16, starting transfers between devices, ring(): r, l = (lax.ppermute(r, Z, right), lax.ppermute(l, Z, left))  28.8 us
    pallas_call x12, Pallas kernels, ring_step(): pl.pallas_call(functools.partial(step_kernel, n, side, first), out_shape=...  16.7 us
    all_to_all x1, starting transfers between devices, on_device(): pieces = lax.all_to_all(pieces, (ROW, XL), 0, 0, tiled=True).reshape(shape)  12.2 us
    pallas_call x1, Pallas kernels, product(): pl.pallas_call(functools.partial(product_kernel, segments), grid=(GRID,),...  9.08 us
    pallas_call x1, Pallas kernels, gather(): pl.pallas_call(functools.partial(gather_kernel, z_n), out_shape=jax.Shape...  3.11 us
    unnamed x4, local copies, waits for them, and re-layouts  3.07 us
    pallas_call x1, Pallas kernels, turn(): pl.pallas_call(functools.partial(turn_kernel, n, rows_n), out_shape=jax.S...  2.57 us
  transfers between devices with their start and end apart: 18, of which 7 were waited for; matrix products, arithmetic and copies ran while one was open for 0% of the time, Pallas kernels for 17%

profile of v4, /device:TPU:1, one launch (start us, length us, event | category | flops | bytes accessed | tf_op | source)
XLA Modules:
  0.0 122.4 jit_solution(16992947022736381052)
XLA Ops:
  0.0 2.4 %copy-done = bf16[100,100,192]{1,2,0:T(8,128)(2,1)S(1)} copy-done((bf16[100,100,192]{1,2,0:T(8,128)(2,1)S(1)}, bf16[100,100,192]{1,2,0:T(8,128)(2,1)}, u32[]{:S(2)}) %copy-start) | copy-done | bytes 3840024
  3.1 3.1 %pick_rows.1.left = bf16[256,192]{1,0:T(8,128)(2,1)S(1)} custom-call(s32[1]{0:T(128)} %bitcast.5.at, s32[2,32]{1,0:T(2,128)S(1)} %bitcast.15, bf16[100,192,100]{2,1,0:T(8,128)(2,1)S(1)} %bitcast.13), custom_call_target="tpu_custom_call" | custom-call | tf_op jit(solution)/shard_map/pick_rows/pallas_call | solution.py:126
  6.2 9.1 %product.1 = (s16[8,16,16512]{2,1,0:T(8,128)(2,1)}, s16[8,16,8320]{2,1,0:T(8,128)(2,1)}, s16[8,16,8320]{2,1,0:T(8,128)(2,1)}, s16[16,8320]{1,0:T(8,128)(2,1)S(1)}, s16[16,8320]{1,0:T(8,128)(2,1)S(1)}) custom-call(s32[1]{0:T(128)} %bitcast.4.at, bf16[256,192]{1,0:T(8,128)(2,1)S(1)} %pick_rows.1.left, bf16[192,16384]{1,0:T(8,128)(2,1)} %right.1), custom_call_target="tpu_custom_call" | custom-call | flops 1610612736 | bytes 14680064 | tf_op jit(solution)/shard_map/product/pallas_call | solution.py:196
  15.3 2.1 %collective-permute-start.8 = (s16[8,16,8320]{2,1,0:T(8,128)(2,1)}, s16[8,16,8320]{2,1,0:T(8,128)(2,1)}, u32[]{:S(2)}, u32[]{:S(2)}) collective-permute-start(s16[8,16,8320]{2,1,0:T(8,128)(2,1)} %get-tuple-element.16), channel_id=1, source_target_pairs={{0,1},{1,0},{2,3},{3,2},{4,5},{5,4},{6,7},{7,6},{8,9},{9,8},{10,11... | collective-permute-start | bytes 6389768 | tf_op jit(solution)/shard_map/ppermute | solution.py:442
  17.4 1.6 %collective-permute-start = (s16[16,8320]{1,0:T(8,128)(2,1)S(1)}, s16[16,8320]{1,0:T(8,128)(2,1)S(1)}, u32[]{:S(2)}, u32[]{:S(2)}) collective-permute-start(s16[16,8320]{1,0:T(8,128)(2,1)S(1)} %get-tuple-element.12), channel_id=1, source_target_pairs={{0,2},{2,4},{4,6},{6,8},{8,10},{10,12},{12,14},{14,0},{1,3},{3,5},... | collective-permute-start | bytes 798728 | tf_op jit(solution)/shard_map/ppermute | solution.py:328
  19.0 3.9 %collective-permute-start.4 = (s16[16,8320]{1,0:T(8,128)(2,1)S(1)}, s16[16,8320]{1,0:T(8,128)(2,1)S(1)}, u32[]{:S(2)}, u32[]{:S(2)}) collective-permute-start(s16[16,8320]{1,0:T(8,128)(2,1)S(1)} %get-tuple-element.14), channel_id=1, source_target_pairs={{2,0},{4,2},{6,4},{8,6},{10,8},{12,10},{14,12},{0,14},{3,1},{5,3},... | collective-permute-start | bytes 798728 | tf_op jit(solution)/shard_map/ppermute | solution.py:328
  23.0 5.8 %collective-permute-done.got = s16[16,8320]{1,0:T(8,128)(2,1)S(1)} collective-permute-done((s16[16,8320]{1,0:T(8,128)(2,1)S(1)}, s16[16,8320]{1,0:T(8,128)(2,1)S(1)}, u32[]{:S(2)}, u32[]{:S(2)}) %collective-permute-start) | collective-permute-done | bytes 266272 | tf_op jit(solution)/shard_map/ppermute | solution.py:328
  28.8 1.4 %ring_step.12.refs_1_ = s16[16,16512]{1,0:T(8,128)(2,1)S(1)} custom-call(s32[1]{0:T(128)} %bitcast.3.at.refs_1_.refs_2_, s16[16,8320]{1,0:T(8,128)(2,1)S(1)} %collective-permute-done.got, s16[8,16,16512]{2,1,0:T(8,128)(2,1)} %get-tuple-element.13.refs_0_.parts, s32[1]{0:T(128)} %bitcast.3.at.refs_1_.refs_2_), custom_call_target="tpu_custom_call" | custom-call | flops 1000 | bytes 3000000 | tf_op jit(solution)/shard_map/ring_step/pallas_call | solution.py:310
  30.3 1.4 %ring_step.15 = s16[16,16512]{1,0:T(8,128)(2,1)S(1)} custom-call(s32[1]{0:T(128)} %bitcast.10.at, s16[16,8320]{1,0:T(8,128)(2,1)S(1)} %collective-permute-done.4.got, s16[8,16,16512]{2,1,0:T(8,128)(2,1)} %get-tuple-element.13.refs_0_.parts, s16[16,16512]{1,0:T(8,128)(2,1)S(1)} %ring_step.12.refs_1_), custom_call_target="tpu_custom_call" | custom-call | flops 1000 | bytes 3000000 | tf_op jit(solution)/shard_map/ring_step/pallas_call | solution.py:310
  31.7 2.7 %collective-permute-start.5 = (s16[16,16512]{1,0:T(8,128)(2,1)S(1)}, s16[16,16512]{1,0:T(8,128)(2,1)S(1)}, u32[]{:S(2)}, u32[]{:S(2)}) collective-permute-start(s16[16,16512]{1,0:T(8,128)(2,1)S(1)} %ring_step.15), channel_id=1, source_target_pairs={{2,0},{4,2},{6,4},{8,6},{10,8},{12,10},{14,12},{0,14},{3,1},{5,3},... | collective-permute-start | bytes 1585160 | tf_op jit(solution)/shard_map/ppermute | solution.py:334
  34.4 9.0 %collective-permute-done.1.got = s16[16,16512]{1,0:T(8,128)(2,1)S(1)} collective-permute-done((s16[16,16512]{1,0:T(8,128)(2,1)S(1)}, s16[16,16512]{1,0:T(8,128)(2,1)S(1)}, u32[]{:S(2)}, u32[]{:S(2)}) %collective-permute-start.1) | collective-permute-done | bytes 528416 | tf_op jit(solution)/shard_map/ppermute | solution.py:334
  43.4 1.5 %ring_step.13.refs_1_ = s16[16,16512]{1,0:T(8,128)(2,1)S(1)} custom-call(s32[1]{0:T(128)} %bitcast.2.at.refs_1_.refs_2_, s16[16,16512]{1,0:T(8,128)(2,1)S(1)} %collective-permute-done.1.got, s16[8,16,16512]{2,1,0:T(8,128)(2,1)} %get-tuple-element.13.refs_0_.parts, s32[1]{0:T(128)} %bitcast.2.at.refs_1_.refs_2_), custom_call_target="tpu_custom_call" | custom-call | flops 1000 | bytes 3000000 | tf_op jit(solution)/shard_map/ring_step/pallas_call | solution.py:310
  45.0 1.5 %ring_step.16 = s16[16,16512]{1,0:T(8,128)(2,1)S(1)} custom-call(s32[1]{0:T(128)} %bitcast.9.at, s16[16,16512]{1,0:T(8,128)(2,1)S(1)} %collective-permute-done.5.got, s16[8,16,16512]{2,1,0:T(8,128)(2,1)} %get-tuple-element.13.refs_0_.parts, s16[16,16512]{1,0:T(8,128)(2,1)S(1)} %ring_step.13.refs_1_), custom_call_target="tpu_custom_call" | custom-call | flops 1000 | bytes 3000000 | tf_op jit(solution)/shard_map/ring_step/pallas_call | solution.py:310
  46.5 2.7 %collective-permute-start.6 = (s16[16,16512]{1,0:T(8,128)(2,1)S(1)}, s16[16,16512]{1,0:T(8,128)(2,1)S(1)}, u32[]{:S(2)}, u32[]{:S(2)}) collective-permute-start(s16[16,16512]{1,0:T(8,128)(2,1)S(1)} %ring_step.16), channel_id=1, source_target_pairs={{2,0},{4,2},{6,4},{8,6},{10,8},{12,10},{14,12},{0,14},{3,1},{5,3},... | collective-permute-start | bytes 1585160 | tf_op jit(solution)/shard_map/ppermute | solution.py:334
  49.2 8.0 %collective-permute-done.2.got = s16[16,16512]{1,0:T(8,128)(2,1)S(1)} collective-permute-done((s16[16,16512]{1,0:T(8,128)(2,1)S(1)}, s16[16,16512]{1,0:T(8,128)(2,1)S(1)}, u32[]{:S(2)}, u32[]{:S(2)}) %collective-permute-start.2) | collective-permute-done | bytes 528416 | tf_op jit(solution)/shard_map/ppermute | solution.py:334
  57.2 1.5 %ring_step.14.refs_1_ = s16[16,16512]{1,0:T(8,128)(2,1)S(1)} custom-call(s32[1]{0:T(128)} %bitcast.1.at.refs_1_.refs_2_, s16[16,16512]{1,0:T(8,128)(2,1)S(1)} %collective-permute-done.2.got, s16[8,16,16512]{2,1,0:T(8,128)(2,1)} %get-tuple-element.13.refs_0_.parts, s32[1]{0:T(128)} %bitcast.1.at.refs_1_.refs_2_), custom_call_target="tpu_custom_call" | custom-call | flops 1000 | bytes 3000000 | tf_op jit(solution)/shard_map/ring_step/pallas_call | solution.py:310
  58.7 1.5 %ring_step.17 = s16[16,16512]{1,0:T(8,128)(2,1)S(1)} custom-call(s32[1]{0:T(128)} %bitcast.8.at, s16[16,16512]{1,0:T(8,128)(2,1)S(1)} %collective-permute-done.6.got, s16[8,16,16512]{2,1,0:T(8,128)(2,1)} %get-tuple-element.13.refs_0_.parts, s16[16,16512]{1,0:T(8,128)(2,1)S(1)} %ring_step.14.refs_1_), custom_call_target="tpu_custom_call" | custom-call | flops 1000 | bytes 3000000 | tf_op jit(solution)/shard_map/ring_step/pallas_call | solution.py:310
  60.2 2.5 %collective-permute-start.7 = (s16[16,16512]{1,0:T(8,128)(2,1)S(1)}, s16[16,16512]{1,0:T(8,128)(2,1)S(1)}, u32[]{:S(2)}, u32[]{:S(2)}) collective-permute-start(s16[16,16512]{1,0:T(8,128)(2,1)S(1)} %ring_step.17), channel_id=1, source_target_pairs={{2,0},{4,2},{6,4},{8,6},{10,8},{12,10},{14,12},{0,14},{3,1},{5,3},... | collective-permute-start | bytes 1585160 | tf_op jit(solution)/shard_map/ppermute | solution.py:334
  64.0 2.7 %collective-permute-start.9 = (s16[16,4224]{1,0:T(8,128)(2,1)S(1)}, s16[16,4224]{1,0:T(8,128)(2,1)S(1)}, u32[]{:S(2)}, u32[]{:S(2)}) collective-permute-start(s16[16,4224]{1,0:T(8,128)(2,1)S(1)} %get-tuple-element.17), channel_id=1, source_target_pairs={{0,2},{2,4},{4,6},{6,8},{8,10},{10,12},{12,14},{14,0},{1,3},{3,5},... | collective-permute-start | bytes 405512 | tf_op jit(solution)/shard_map/ppermute | solution.py:328
  66.7 4.2 %collective-permute-start.13 = (s16[16,4224]{1,0:T(8,128)(2,1)S(1)}, s16[16,4224]{1,0:T(8,128)(2,1)S(1)}, u32[]{:S(2)}, u32[]{:S(2)}) collective-permute-start(s16[16,4224]{1,0:T(8,128)(2,1)S(1)} %get-tuple-element.18), channel_id=1, source_target_pairs={{2,0},{4,2},{6,4},{8,6},{10,8},{12,10},{14,12},{0,14},{3,1},{5,3},... | collective-permute-start | bytes 405512 | tf_op jit(solution)/shard_map/ppermute | solution.py:328
  70.9 5.5 %collective-permute-done.9.got = s16[16,4224]{1,0:T(8,128)(2,1)S(1)} collective-permute-done((s16[16,4224]{1,0:T(8,128)(2,1)S(1)}, s16[16,4224]{1,0:T(8,128)(2,1)S(1)}, u32[]{:S(2)}, u32[]{:S(2)}) %collective-permute-start.9) | collective-permute-done | bytes 135200 | tf_op jit(solution)/shard_map/ppermute | solution.py:328
  79.1 2.7 %collective-permute-start.14 = (s16[16,8320]{1,0:T(8,128)(2,1)S(1)}, s16[16,8320]{1,0:T(8,128)(2,1)S(1)}, u32[]{:S(2)}, u32[]{:S(2)}) collective-permute-start(s16[16,8320]{1,0:T(8,128)(2,1)S(1)} %ring_step.21), channel_id=1, source_target_pairs={{2,0},{4,2},{6,4},{8,6},{10,8},{12,10},{14,12},{0,14},{3,1},{5,3},... | collective-permute-start | bytes 798728 | tf_op jit(solution)/shard_map/ppermute | solution.py:334
  81.9 2.6 %turn.1 = s16[16,2,80,128]{3,2,1,0:T(8,128)(2,1)} custom-call(s32[1]{0:T(128)} %bitcast.at, s16[16,16512]{1,0:T(8,128)(2,1)S(1)} %collective-permute-done.3.got_r, s16[16,16512]{1,0:T(8,128)(2,1)S(1)} %collective-permute-done.7.got_l, s16[8,16,16512]{2,1,0:T(8,128)(2,1)} %get-tuple-element.13.refs_0_.parts), custom_call_target="tpu_custom_call" | custom-call | flops 2113536 | bytes 2113536 | tf_op jit(solution)/shard_map/turn/pallas_call | solution.py:367
  84.4 12.2 %all-to-all-start = ((s16[32,80,128]{2,1,0:T(8,128)(2,1)}), s16[32,80,128]{2,1,0:T(8,128)(2,1)S(1)}, u32[]{:S(2)}, u32[]{:S(2)}) async-start(s16[32,80,128]{2,1,0:T(8,128)(2,1)} %bitcast.11), calls=%async_computation | async-start | bytes 1310720 | tf_op jit(solution)/shard_map/all_to_all | solution.py:447
  96.7 1.3 %ring_step.19.refs_2_ = s16[16,8320]{1,0:T(8,128)(2,1)S(1)} custom-call(s32[1]{0:T(128)} %bitcast.2.at.refs_1_.refs_2_, s16[16,8320]{1,0:T(8,128)(2,1)S(1)} %collective-permute-done.10.got, s16[8,16,8320]{2,1,0:T(8,128)(2,1)} %get-tuple-element.15.refs_0_, s16[8,16,8320]{2,1,0:T(8,128)(2,1)} %collective-permute-done.8.refs_1_, s32[1]{0:T(128)} %bitcast.2.at.refs_1_.refs_2_), custom_call_target="tpu_custom_call" | custom-call | flops 1000 | bytes 3000000 | tf_op jit(solution)/shard_map/ring_step/pallas_call | solution.py:310
  98.1 1.3 %ring_step.22 = s16[16,8320]{1,0:T(8,128)(2,1)S(1)} custom-call(s32[1]{0:T(128)} %bitcast.9.at, s16[16,8320]{1,0:T(8,128)(2,1)S(1)} %collective-permute-done.14.got, s16[8,16,8320]{2,1,0:T(8,128)(2,1)} %get-tuple-element.15.refs_0_, s16[8,16,8320]{2,1,0:T(8,128)(2,1)} %collective-permute-done.8.refs_1_, s16[16,8320]{1,0:T(8,128)(2,1)S(1)} %ring_step.19.refs_2_), custom_call_target="tpu_custom_call" | custom-call | flops 1000 | bytes 3000000 | tf_op jit(solution)/shard_map/ring_step/pallas_call | solution.py:310
  99.5 2.7 %collective-permute-start.15 = (s16[16,8320]{1,0:T(8,128)(2,1)S(1)}, s16[16,8320]{1,0:T(8,128)(2,1)S(1)}, u32[]{:S(2)}, u32[]{:S(2)}) collective-permute-start(s16[16,8320]{1,0:T(8,128)(2,1)S(1)} %ring_step.22), channel_id=1, source_target_pairs={{2,0},{4,2},{6,4},{8,6},{10,8},{12,10},{14,12},{0,14},{3,1},{5,3},... | collective-permute-start | bytes 798728 | tf_op jit(solution)/shard_map/ppermute | solution.py:334
  102.2 4.9 %collective-permute-done.11.got = s16[16,8320]{1,0:T(8,128)(2,1)S(1)} collective-permute-done((s16[16,8320]{1,0:T(8,128)(2,1)S(1)}, s16[16,8320]{1,0:T(8,128)(2,1)S(1)}, u32[]{:S(2)}, u32[]{:S(2)}) %collective-permute-start.11) | collective-permute-done | bytes 266272 | tf_op jit(solution)/shard_map/ppermute | solution.py:334
  109.8 2.5 %collective-permute-start.16 = (s16[16,8320]{1,0:T(8,128)(2,1)S(1)}, s16[16,8320]{1,0:T(8,128)(2,1)S(1)}, u32[]{:S(2)}, u32[]{:S(2)}) collective-permute-start(s16[16,8320]{1,0:T(8,128)(2,1)S(1)} %ring_step.23), channel_id=1, source_target_pairs={{2,0},{4,2},{6,4},{8,6},{10,8},{12,10},{14,12},{0,14},{3,1},{5,3},... | collective-permute-start | bytes 798728 | tf_op jit(solution)/shard_map/ppermute | solution.py:334
  112.3 4.4 %collective-permute-done.16.l = s16[16,8320]{1,0:T(8,128)(2,1)S(1)} collective-permute-done((s16[16,8320]{1,0:T(8,128)(2,1)S(1)}, s16[16,8320]{1,0:T(8,128)(2,1)S(1)}, u32[]{:S(2)}, u32[]{:S(2)}) %collective-permute-start.16) | collective-permute-done | bytes 266272 | tf_op jit(solution)/shard_map/ppermute | solution.py:334
  116.7 3.0 %collective-permute-done.12.r = s16[16,8320]{1,0:T(8,128)(2,1)S(1)} collective-permute-done((s16[16,8320]{1,0:T(8,128)(2,1)S(1)}, s16[16,8320]{1,0:T(8,128)(2,1)S(1)}, u32[]{:S(2)}, u32[]{:S(2)}) %collective-permute-start.12) | collective-permute-done | bytes 266272 | tf_op jit(solution)/shard_map/ppermute | solution.py:334
  119.7 2.5 %last.1 = bf16[8,16384]{1,0:T(8,128)(2,1)} custom-call(s32[1]{0:T(128)} %bitcast.at, s16[16,2,80,128]{3,2,1,0:T(8,128)(2,1)S(1)} %bitcast.14, s16[16,8320]{1,0:T(8,128)(2,1)S(1)} %collective-permute-done.12.r, s16[16,8320]{1,0:T(8,128)(2,1)S(1)} %collective-permute-done.16.l, s16[8,16,8320]{2,1,0:T(8,128)(2,1)} %get-tuple-element.15.refs_0_, ...), custom_call_target="tpu_custom_call" | custom-call | tf_op jit(solution)/shard_map/last/pallas_call | solution.py:427
  (25 shorter events, 7.6 us)
Async XLA Ops:
  0.0 2.4 %copy-start = (bf16[100,100,192]{1,2,0:T(8,128)(2,1)S(1)}, bf16[100,100,192]{1,2,0:T(8,128)(2,1)}, u32[]{:S(2)}) copy-start(bf16[100,100,192]{1,2,0:T(8,128)(2,1)} %param.3) | copy-start | bytes 11520004
  2.4 0.7 copy-start.1
  15.3 47.5 %collective-permute-start.8 = (s16[8,16,8320]{2,1,0:T(8,128)(2,1)}, s16[8,16,8320]{2,1,0:T(8,128)(2,1)}, u32[]{:S(2)}, u32[]{:S(2)}) collective-permute-start(s16[8,16,8320]{2,1,0:T(8,128)(2,1)} %get-tuple-element.16), channel_id=1, source_target_pairs={{0,1},{1,0},{2,3},{3,2},{4,5},{5,4},{6,7},{7,6},{8,9},{9,8},{10,11... | collective-permute-start | bytes 6389768 | tf_op jit(solution)/shard_map/ppermute | solution.py:442
  17.4 11.4 %collective-permute-start = (s16[16,8320]{1,0:T(8,128)(2,1)S(1)}, s16[16,8320]{1,0:T(8,128)(2,1)S(1)}, u32[]{:S(2)}, u32[]{:S(2)}) collective-permute-start(s16[16,8320]{1,0:T(8,128)(2,1)S(1)} %get-tuple-element.12), channel_id=1, source_target_pairs={{0,2},{2,4},{4,6},{6,8},{8,10},{10,12},{12,14},{14,0},{1,3},{3,5},... | collective-permute-start | bytes 798728 | tf_op jit(solution)/shard_map/ppermute | solution.py:328
  19.0 11.2 %collective-permute-start.4 = (s16[16,8320]{1,0:T(8,128)(2,1)S(1)}, s16[16,8320]{1,0:T(8,128)(2,1)S(1)}, u32[]{:S(2)}, u32[]{:S(2)}) collective-permute-start(s16[16,8320]{1,0:T(8,128)(2,1)S(1)} %get-tuple-element.14), channel_id=1, source_target_pairs={{2,0},{4,2},{6,4},{8,6},{10,8},{12,10},{14,12},{0,14},{3,1},{5,3},... | collective-permute-start | bytes 798728 | tf_op jit(solution)/shard_map/ppermute | solution.py:328
  30.2 13.2 %collective-permute-start.1 = (s16[16,16512]{1,0:T(8,128)(2,1)S(1)}, s16[16,16512]{1,0:T(8,128)(2,1)S(1)}, u32[]{:S(2)}, u32[]{:S(2)}) collective-permute-start(s16[16,16512]{1,0:T(8,128)(2,1)S(1)} %ring_step.12.refs_1_), channel_id=1, source_target_pairs={{0,2},{2,4},{4,6},{6,8},{8,10},{10,12},{12,14},{14,0},{1,3},{3,5},... | collective-permute-start | bytes 1585160 | tf_op jit(solution)/shard_map/ppermute | solution.py:334
  31.7 13.3 %collective-permute-start.5 = (s16[16,16512]{1,0:T(8,128)(2,1)S(1)}, s16[16,16512]{1,0:T(8,128)(2,1)S(1)}, u32[]{:S(2)}, u32[]{:S(2)}) collective-permute-start(s16[16,16512]{1,0:T(8,128)(2,1)S(1)} %ring_step.15), channel_id=1, source_target_pairs={{2,0},{4,2},{6,4},{8,6},{10,8},{12,10},{14,12},{0,14},{3,1},{5,3},... | collective-permute-start | bytes 1585160 | tf_op jit(solution)/shard_map/ppermute | solution.py:334
  44.9 12.3 %collective-permute-start.2 = (s16[16,16512]{1,0:T(8,128)(2,1)S(1)}, s16[16,16512]{1,0:T(8,128)(2,1)S(1)}, u32[]{:S(2)}, u32[]{:S(2)}) collective-permute-start(s16[16,16512]{1,0:T(8,128)(2,1)S(1)} %ring_step.13.refs_1_), channel_id=1, source_target_pairs={{0,2},{2,4},{4,6},{6,8},{8,10},{10,12},{12,14},{14,0},{1,3},{3,5},... | collective-permute-start | bytes 1585160 | tf_op jit(solution)/shard_map/ppermute | solution.py:334
  46.5 12.2 %collective-permute-start.6 = (s16[16,16512]{1,0:T(8,128)(2,1)S(1)}, s16[16,16512]{1,0:T(8,128)(2,1)S(1)}, u32[]{:S(2)}, u32[]{:S(2)}) collective-permute-start(s16[16,16512]{1,0:T(8,128)(2,1)S(1)} %ring_step.16), channel_id=1, source_target_pairs={{2,0},{4,2},{6,4},{8,6},{10,8},{12,10},{14,12},{0,14},{3,1},{5,3},... | collective-permute-start | bytes 1585160 | tf_op jit(solution)/shard_map/ppermute | solution.py:334
  60.2 21.7 %collective-permute-start.7 = (s16[16,16512]{1,0:T(8,128)(2,1)S(1)}, s16[16,16512]{1,0:T(8,128)(2,1)S(1)}, u32[]{:S(2)}, u32[]{:S(2)}) collective-permute-start(s16[16,16512]{1,0:T(8,128)(2,1)S(1)} %ring_step.17), channel_id=1, source_target_pairs={{2,0},{4,2},{6,4},{8,6},{10,8},{12,10},{14,12},{0,14},{3,1},{5,3},... | collective-permute-start | bytes 1585160 | tf_op jit(solution)/shard_map/ppermute | solution.py:334
  62.7 19.1 %collective-permute-start.3 = (s16[16,16512]{1,0:T(8,128)(2,1)S(1)}, s16[16,16512]{1,0:T(8,128)(2,1)S(1)}, u32[]{:S(2)}, u32[]{:S(2)}) collective-permute-start(s16[16,16512]{1,0:T(8,128)(2,1)S(1)} %ring_step.14.refs_1_), channel_id=1, source_target_pairs={{0,2},{2,4},{4,6},{6,8},{8,10},{10,12},{12,14},{14,0},{1,3},{3,5},... | collective-permute-start | bytes 1585160 | tf_op jit(solution)/shard_map/ppermute | solution.py:334
  64.0 12.4 %collective-permute-start.9 = (s16[16,4224]{1,0:T(8,128)(2,1)S(1)}, s16[16,4224]{1,0:T(8,128)(2,1)S(1)}, u32[]{:S(2)}, u32[]{:S(2)}) collective-permute-start(s16[16,4224]{1,0:T(8,128)(2,1)S(1)} %get-tuple-element.17), channel_id=1, source_target_pairs={{0,2},{2,4},{4,6},{6,8},{8,10},{10,12},{12,14},{14,0},{1,3},{3,5},... | collective-permute-start | bytes 405512 | tf_op jit(solution)/shard_map/ppermute | solution.py:328
  66.7 11.1 %collective-permute-start.13 = (s16[16,4224]{1,0:T(8,128)(2,1)S(1)}, s16[16,4224]{1,0:T(8,128)(2,1)S(1)}, u32[]{:S(2)}, u32[]{:S(2)}) collective-permute-start(s16[16,4224]{1,0:T(8,128)(2,1)S(1)} %get-tuple-element.18), channel_id=1, source_target_pairs={{2,0},{4,2},{6,4},{8,6},{10,8},{12,10},{14,12},{0,14},{3,1},{5,3},... | collective-permute-start | bytes 405512 | tf_op jit(solution)/shard_map/ppermute | solution.py:328
  77.7 18.9 %collective-permute-start.10 = (s16[16,8320]{1,0:T(8,128)(2,1)S(1)}, s16[16,8320]{1,0:T(8,128)(2,1)S(1)}, u32[]{:S(2)}, u32[]{:S(2)}) collective-permute-start(s16[16,8320]{1,0:T(8,128)(2,1)S(1)} %ring_step.18.refs_2_), channel_id=1, source_target_pairs={{0,2},{2,4},{4,6},{6,8},{8,10},{10,12},{12,14},{14,0},{1,3},{3,5},... | collective-permute-start | bytes 798728 | tf_op jit(solution)/shard_map/ppermute | solution.py:334
  79.1 19.0 %collective-permute-start.14 = (s16[16,8320]{1,0:T(8,128)(2,1)S(1)}, s16[16,8320]{1,0:T(8,128)(2,1)S(1)}, u32[]{:S(2)}, u32[]{:S(2)}) collective-permute-start(s16[16,8320]{1,0:T(8,128)(2,1)S(1)} %ring_step.21), channel_id=1, source_target_pairs={{2,0},{4,2},{6,4},{8,6},{10,8},{12,10},{14,12},{0,14},{3,1},{5,3},... | collective-permute-start | bytes 798728 | tf_op jit(solution)/shard_map/ppermute | solution.py:334
  84.4 27.8 %all-to-all-start = ((s16[32,80,128]{2,1,0:T(8,128)(2,1)}), s16[32,80,128]{2,1,0:T(8,128)(2,1)S(1)}, u32[]{:S(2)}, u32[]{:S(2)}) async-start(s16[32,80,128]{2,1,0:T(8,128)(2,1)} %bitcast.11), calls=%async_computation | async-start | bytes 1310720 | tf_op jit(solution)/shard_map/all_to_all | solution.py:447
  98.0 9.1 %collective-permute-start.11 = (s16[16,8320]{1,0:T(8,128)(2,1)S(1)}, s16[16,8320]{1,0:T(8,128)(2,1)S(1)}, u32[]{:S(2)}, u32[]{:S(2)}) collective-permute-start(s16[16,8320]{1,0:T(8,128)(2,1)S(1)} %ring_step.19.refs_2_), channel_id=1, source_target_pairs={{0,2},{2,4},{4,6},{6,8},{8,10},{10,12},{12,14},{14,0},{1,3},{3,5},... | collective-permute-start | bytes 798728 | tf_op jit(solution)/shard_map/ppermute | solution.py:334
  99.5 8.9 %collective-permute-start.15 = (s16[16,8320]{1,0:T(8,128)(2,1)S(1)}, s16[16,8320]{1,0:T(8,128)(2,1)S(1)}, u32[]{:S(2)}, u32[]{:S(2)}) collective-permute-start(s16[16,8320]{1,0:T(8,128)(2,1)S(1)} %ring_step.22), channel_id=1, source_target_pairs={{2,0},{4,2},{6,4},{8,6},{10,8},{12,10},{14,12},{0,14},{3,1},{5,3},... | collective-permute-start | bytes 798728 | tf_op jit(solution)/shard_map/ppermute | solution.py:334
  109.8 6.9 %collective-permute-start.16 = (s16[16,8320]{1,0:T(8,128)(2,1)S(1)}, s16[16,8320]{1,0:T(8,128)(2,1)S(1)}, u32[]{:S(2)}, u32[]{:S(2)}) collective-permute-start(s16[16,8320]{1,0:T(8,128)(2,1)S(1)} %ring_step.23), channel_id=1, source_target_pairs={{2,0},{4,2},{6,4},{8,6},{10,8},{12,10},{14,12},{0,14},{3,1},{5,3},... | collective-permute-start | bytes 798728 | tf_op jit(solution)/shard_map/ppermute | solution.py:334
  112.3 7.5 %collective-permute-start.12 = (s16[16,8320]{1,0:T(8,128)(2,1)S(1)}, s16[16,8320]{1,0:T(8,128)(2,1)S(1)}, u32[]{:S(2)}, u32[]{:S(2)}) collective-permute-start(s16[16,8320]{1,0:T(8,128)(2,1)S(1)} %ring_step.20.refs_2_), channel_id=1, source_target_pairs={{0,2},{2,4},{4,6},{6,8},{8,10},{10,12},{12,14},{14,0},{1,3},{3,5},... | collective-permute-start | bytes 798728 | tf_op jit(solution)/shard_map/ppermute | solution.py:334
